TPU v7x, 128 devices: a whole 4x4x4 slice. The times are simulated.
128 devices in a mesh: dp: 4 (over y), expert: 32 (over z, x, core).
Axes of the slice: x: 4, y: 4, z: 4, core: 2. Of those that a mesh axis runs over, the one named last changes fastest.
Arguments:
- grad_out: bfloat16 [32768, 4096], P(('dp', 'expert')), may hold values from -6 to 6
- expert_ids: int32 [32768, 8], P(('dp', 'expert')), may hold values from 0 to 63, all different within a row; in each aligned block of 256 rows (0 to 255, 256 to 511, ...) at most 36 rows name the same one
- route_weights: bfloat16 [32768, 8], P(('dp', 'expert')), may hold values from 0.099609375 to 1
- gate_values: bfloat16 [4, 64, 1152, 768], P('dp', 'expert'), may hold values from -5 to 5
- up_values: bfloat16 [4, 64, 1152, 768], P('dp', 'expert'), may hold values from -5 to 5
- w_down: bfloat16 [64, 768, 4096], P('expert', None, 'dp'), as said below
Outputs:
- grad_gate: bfloat16 [4, 64, 1152, 768], P('dp', 'expert')
- grad_up: bfloat16 [4, 64, 1152, 768], P('dp', 'expert')
- grad_down: bfloat16 [64, 768, 4096], P('expert', None, 'dp')
- grad_route: float32 [32768, 8], P(('dp', 'expert'))
Inputs may be any that keep to these rules, and one draw needn't show every extreme that they name: `expert_ids`: each token names 8 different experts. Among the tokens of one device no expert is named by more than 36 tokens, a bound that some block reaches. `w_down`: rows of the experts' weights and its columns have different scales.
All inputs are finite; a program needn't handle non-finite values.
Results may differ from a plain program's by a relative error of at most 0.015.
Values may be sent and summed in bfloat16 or wider, within the bound.
No kernel may reach another device: no remote copies, remote signals or barrier semaphores. Data moves between devices by JAX's collectives and lax.ppermute only.
A program may use at most 256 MiB of HBM per device.

v0:
```python
import functools

import jax
import jax.numpy as jnp
from jax import lax
from jax.experimental import pallas as pl
from jax.experimental.pallas import tpu as pltpu
from jax.sharding import PartitionSpec as P

epsilon = 1e-06

D = 4096
H = 768
TOP = 8
TOK = 256
CAP = 36
SLOTS = 1152
NZ = NX = 4
NDP = 4
PART = 2 * CAP
SEG = NZ * PART
UNIT = 256
HALF = 2 * UNIT
WIDE = NDP * HALF
SHIFTS = (0, 1, 3, 2)
VMEM_LIMIT = 56 * 1024 * 1024


def member(z, x, core):
    return ((z % NZ) * NX + (x % NX)) * 2 + core


def pairs(first_axis, shift, swap):
    out = []
    for z in range(NZ):
        for x in range(NX):
            for core in range(2):
                along_z = (core == 0) == first_axis
                to = (z + shift, x) if along_z else (z, x + shift)
                out.append((member(z, x, core), member(*to, core ^ swap)))
    return out


def params(**kw):
    return pltpu.CompilerParams(vmem_limit_bytes=VMEM_LIMIT, **kw)


def cost(flops, nbytes, trans=0):
    return pl.CostEstimate(flops=int(flops), bytes_accessed=int(nbytes), transcendentals=int(trans))


def shrink_kernel(half_ref, w_ref, out_ref, sums_ref):
    dense = w_ref[0].astype(jnp.float32).reshape(H // 8, 8, UNIT)
    row = lax.broadcasted_iota(jnp.int32, dense.shape, 1)
    odd = (row & 1) == 1
    high = (row & 2) == 2

    def across(value, step, upper):
        return jnp.where(upper, pltpu.roll(value, step, 1), pltpu.roll(value, 8 - step, 1))

    mag = jnp.abs(dense)
    other = across(mag, 1, odd)
    low, up = jnp.minimum(mag, other), jnp.maximum(mag, other)
    second = jnp.minimum(
        jnp.maximum(low, across(low, 2, high)), jnp.minimum(up, across(up, 2, high))
    )
    kept = jnp.maximum(mag - second, 0.0)
    shrunk = jnp.where(dense < 0.0, -kept, kept)
    out_ref[...] = shrunk.reshape(out_ref.shape).astype(jnp.bfloat16)

    def fold(value):
        value = jnp.sum(value, axis=0)
        return value[:, :128] + value[:, 128:]

    sums_ref[0, 0, 0] = fold(dense * shrunk)
    sums_ref[0, 0, 1] = fold(shrunk * shrunk)


def shrink(half, wide, w_down):
    if wide:
        spec = pl.BlockSpec((1, 1, H, UNIT), lambda e, t, s: (1, e, 0, t))
        shape = jax.ShapeDtypeStruct((2, 2, H, HALF), jnp.bfloat16)
    else:
        spec = pl.BlockSpec((1, H, UNIT), lambda e, t, s: (e, 0, t))
        shape = jax.ShapeDtypeStruct((2, H, HALF), jnp.bfloat16)
    return pl.pallas_call(
        shrink_kernel,
        grid_spec=pltpu.PrefetchScalarGridSpec(
            num_scalar_prefetch=1,
            grid=(2, 2),
            in_specs=[pl.BlockSpec((1, H, UNIT), lambda e, t, s: (e, 0, 2 * s[0] + t))],
            out_specs=[spec, pl.BlockSpec((1, 1, 2, 8, 128), lambda e, t, s: (t, e, 0, 0, 0))],
        ),
        out_shape=[shape, jax.ShapeDtypeStruct((2, 2, 2, 8, 128), jnp.float32)],
        compiler_params=params(),
        cost_estimate=cost(2 * H * HALF * 30, 2 * 2 * H * HALF * 2),
        name="shrink",
    )(half.reshape(1).astype(jnp.int32), w_down)


def back_kernel(ids_ref, rank_ref, score_ref, out_ref):
    expert = lax.broadcasted_iota(jnp.int32, (64, TOK), 0)
    rank = rank_ref[...]
    score = jnp.zeros((64, TOK), jnp.float32)
    for slot in range(CAP):
        score = jnp.where(rank == float(slot), score_ref[:, slot : slot + 1], score)
    for k in range(TOP):
        hit = ids_ref[k : k + 1, :] == expert
        out_ref[k : k + 1, :] = jnp.sum(jnp.where(hit, score, 0.0), axis=0, keepdims=True)


def back(ids, rank, score):
    out = pl.pallas_call(
        back_kernel,
        out_shape=jax.ShapeDtypeStruct((TOP, TOK), jnp.float32),
        compiler_params=params(),
        name="back",
    )(ids.T, rank, score)
    return out.T


def split_kernel(core_ref, rows_ref, ids_ref, weights_ref, mine_ref, theirs_ref, share_ref, rank_ref):
    core = core_ref[0]
    owner = pl.program_id(0)

    @pl.when(owner == 0)
    def _():
        expert = lax.broadcasted_iota(jnp.int32, (64, TOK), 0)
        named = jnp.zeros((64, TOK), jnp.float32)
        weight = jnp.zeros((64, TOK), jnp.float32)
        for k in range(TOP):
            hit = ids_ref[k : k + 1, :] == expert
            named = jnp.where(hit, 1.0, named)
            weight = jnp.where(hit, weights_ref[k : k + 1, :], weight)
        earlier = lax.broadcasted_iota(jnp.int32, (TOK, TOK), 0) < lax.broadcasted_iota(
            jnp.int32, (TOK, TOK), 1
        )
        rank = jnp.dot(
            named.astype(jnp.bfloat16),
            jnp.where(earlier, 1.0, 0.0).astype(jnp.bfloat16),
            preferred_element_type=jnp.float32,
        )
        rank = jnp.where(named > 0.0, rank, -1.0)
        rank_ref[...] = rank
        lane = lax.broadcasted_iota(jnp.int32, (64, 128), 1)
        share = jnp.zeros((64, 128), jnp.float32)
        for slot in range(CAP):
            one = jnp.sum(jnp.where(rank == float(slot), weight, 0.0), axis=1, keepdims=True)
            share = jnp.where(lane == slot, one, share)
        share_ref[...] = share.astype(jnp.bfloat16)

    ranks = rank_ref[pl.ds(pl.multiple_of(owner * 16, 16), 16), :].astype(jnp.bfloat16)
    ranks = jnp.concatenate([ranks, jnp.zeros_like(ranks)], axis=1)
    columns = lambda half: pl.ds(pl.multiple_of(half * HALF, HALF), HALF)
    mine_ref[0, :TOK, :] = rows_ref[:, columns(core)]
    theirs_ref[:TOK, :] = rows_ref[:, columns(1 - core)]
    mine_ref[0, TOK:, :] = ranks
    theirs_ref[TOK:, :] = ranks


def split(core, rows, ids, weights):
    deep = TOK + 16
    small = pl.BlockSpec((TOP, TOK), lambda j, s: (0, 0))
    return pl.pallas_call(
        split_kernel,
        grid_spec=pltpu.PrefetchScalarGridSpec(
            num_scalar_prefetch=1,
            grid=(NDP,),
            in_specs=[pl.BlockSpec((TOK, 1024), lambda j, s: (0, j)), small, small],
            out_specs=[
                pl.BlockSpec((1, deep, HALF), lambda j, s: (s[0], 0, j)),
                pl.BlockSpec((deep, HALF), lambda j, s: (0, j)),
                pl.BlockSpec((64, 128), lambda j, s: (0, 0)),
                pl.BlockSpec((64, TOK), lambda j, s: (0, 0)),
            ],
        ),
        out_shape=[
            jax.ShapeDtypeStruct((2, deep, WIDE), jnp.bfloat16),
            jax.ShapeDtypeStruct((deep, WIDE), jnp.bfloat16),
            jax.ShapeDtypeStruct((64, 128), jnp.bfloat16),
            jax.ShapeDtypeStruct((64, TOK), jnp.float32),
        ],
        compiler_params=params(),
        name="split",
    )(core.reshape(1).astype(jnp.int32), rows, ids.T, weights.astype(jnp.float32).T)


def pick_kernel(swap, where_ref, *refs):
    outs = refs[5:9]
    tokens, coded, ranks, onehot, picked, sems = refs[9:]
    blocks = [[ref.at[part] for part in range(2)] for ref in refs[:3]] + [refs[3:5]]
    step = pl.program_id(0)
    core = where_ref[8]

    def tile(n):
        columns = pl.ds(pl.multiple_of(n * HALF, HALF), HALF)
        return [
            pltpu.make_async_copy(
                blocks[i][part].at[pl.ds(0, TOK), columns],
                tokens.at[n, where_ref[i], pl.ds(part * TOK, TOK)],
                sems.at[n, 2 * i + part],
            )
            for i in range(4)
            for part in range(2)
        ]

    @pl.when(step == 0)
    def _():
        plane = [jnp.where(core == 0, where_ref[9], where_ref[4 + i]) for i in range(4)]
        inside = [jnp.where(core == 0, where_ref[4 + i], where_ref[9]) for i in range(4)]
        tables = [
            pltpu.make_async_copy(
                blocks[i][part].at[pl.ds(TOK, 16)], coded.at[where_ref[i], part], sems.at[4, 2 * i + part]
            )
            for i in range(4)
            for part in range(2)
        ]
        for copy in tables:
            copy.start()
        for n in range(4):
            for copy in tile(n):
                copy.start()
        for copy in tables:
            copy.wait()
        for block in range(4):
            for part in range(2):
                ranks[block, part] = coded[block, part].astype(jnp.float32)
        row = lax.broadcasted_iota(jnp.int32, (PART, 2 * TOK), 0)
        lane = lax.broadcasted_iota(jnp.int32, (PART, 2 * TOK), 1)
        second = row >= CAP
        slot = jnp.where(second, row - CAP, row)
        slot = jnp.where(second == (lane >= TOK), slot, -2).astype(jnp.float32)
        for i in range(8):
            to, e = i // 2, i % 2
            at = inside[to] * 4 + jnp.where(core == swap, 0, 2) + e
            columns = pl.ds(pl.multiple_of(plane[to] * HALF, HALF), TOK)
            for block in range(4):
                rank = jnp.concatenate(
                    [ranks[block, part, pl.ds(at, 1), columns] for part in range(2)], axis=1
                )
                onehot[block, i * PART : (i + 1) * PART, :] = jnp.where(
                    slot == rank, 1.0, 0.0
                ).astype(jnp.bfloat16)

    for copy in tile(step):
        copy.wait()
    for block in range(4):
        picked[block] = jnp.dot(
            onehot[block], tokens[step, block], preferred_element_type=jnp.float32
        )
    for i in range(8):
        rows = pl.ds(i * PART, PART)
        joined = jnp.concatenate([picked[block, rows, :] for block in range(4)], axis=0)
        outs[i // 2][i % 2] = joined.astype(jnp.bfloat16)


def pick(swap, where, blocks):
    any_spec = pl.BlockSpec(memory_space=pl.ANY)
    return pl.pallas_call(
        functools.partial(pick_kernel, swap),
        grid_spec=pltpu.PrefetchScalarGridSpec(
            num_scalar_prefetch=1,
            grid=(4,),
            in_specs=[any_spec] * 5,
            out_specs=[pl.BlockSpec((2, SEG, HALF), lambda n, s: (0, 0, n))] * 4,
            scratch_shapes=[
                pltpu.VMEM((4, 4, 2 * TOK, HALF), jnp.bfloat16),
                pltpu.VMEM((4, 2, 16, WIDE), jnp.bfloat16),
                pltpu.VMEM((4, 2, 16, WIDE), jnp.float32),
                pltpu.VMEM((4, 8 * PART, 2 * TOK), jnp.bfloat16),
                pltpu.VMEM((4, 8 * PART, HALF), jnp.float32),
                pltpu.SemaphoreType.DMA((5, 8)),
            ],
        ),
        out_shape=[jax.ShapeDtypeStruct((2, SEG, WIDE), jnp.bfloat16)] * 4,
        compiler_params=params(),
        cost_estimate=cost(2 * 4 * 576 * 512 * WIDE, 8 * TOK * WIDE * 2 + 8 * SEG * WIDE * 2),
        name=f"pick{1 - swap}",
    )(where, *blocks)


def weigh_kernel(core_ref, gate_ref, up_ref, weight_ref, mine_ref, theirs_ref):
    gate = gate_ref[0].astype(jnp.float32)
    up = up_ref[0].astype(jnp.float32)
    sig = 0.5 * jnp.tanh(0.5 * gate) + 0.5
    value = weight_ref[0] * (gate * sig * up)
    turned = jnp.concatenate(
        [
            value[(z * NX + x) * PART : (z * NX + x + 1) * PART]
            for x in range(NX)
            for z in range(NZ)
        ],
        axis=0,
    )
    plain, turned = value.astype(jnp.bfloat16).T, turned.astype(jnp.bfloat16).T

    @pl.when(core_ref[0] == 0)
    def _():
        mine_ref[0] = turned
        theirs_ref[0] = plain

    @pl.when(core_ref[0] == 1)
    def _():
        mine_ref[0] = plain
        theirs_ref[0] = turned


def weigh(core, gate, up, slot_weight):
    wide = 256
    column = pl.BlockSpec((1, SLOTS, wide), lambda e, n, s: (e, 0, n))
    out = pl.BlockSpec((1, wide, SLOTS), lambda e, n, s: (e, n, 0))
    return pl.pallas_call(
        weigh_kernel,
        grid_spec=pltpu.PrefetchScalarGridSpec(
            num_scalar_prefetch=1,
            grid=(2, H // wide),
            in_specs=[column, column, pl.BlockSpec((1, SLOTS, 1), lambda e, n, s: (e, 0, 0))],
            out_specs=[out, out],
        ),
        out_shape=[jax.ShapeDtypeStruct((2, H, SLOTS), jnp.bfloat16)] * 2,
        compiler_params=params(),
        cost_estimate=cost(2 * SLOTS * H * 20, 2 * SLOTS * H * 8, 2 * SLOTS * H),
        name="weigh",
    )(core.reshape(1).astype(jnp.int32), gate, up, slot_weight)


OWNERS = (0, 1, 3, 2)
DEPTH = 3


def segment(where_ref, i):
    return pl.ds(pl.multiple_of(where_ref[i] * SEG, SEG), SEG)


def partial_kernel(ring, where_ref, weighted_ref, *refs):
    buffers, outs = refs[:4], refs[4:-6]
    weights, rows, ready, weight_sems, in_sems, out_sems = refs[-6:]
    steps = [(i, j) for i in range(2) for j in (3, 1, 2, 0)]

    def load(s):
        i, j = steps[s]
        at = lax.rem(where_ref[5] + OWNERS[j], NDP) if ring else j
        columns = pl.ds(pl.multiple_of(at * HALF, HALF), HALF)
        return [
            pltpu.make_async_copy(
                buffers[r].at[i, :, columns],
                rows.at[s % DEPTH, segment(where_ref, r)],
                in_sems.at[s % DEPTH, r],
            )
            for r in range(4)
        ]

    def store(s):
        i, j = steps[s]
        if ring:
            own, up_first, down_first, up_last, down_last = outs
            to = {
                0: [own.at[0, i], own.at[1, i]],
                1: [up_last.at[i], up_first.at[1, i]],
                2: [down_first.at[0, i], down_last.at[i]],
                3: [up_first.at[0, i], down_first.at[1, i]],
            }[j]
        else:
            to = [outs[0].at[j, p, i] for p in range(2)]
        return [
            pltpu.make_async_copy(ready.at[s % 2, p], to[p], out_sems.at[s % 2, p]) for p in range(2)
        ]

    fetch = [
        pltpu.make_async_copy(weighted_ref.at[i], weights.at[i], weight_sems.at[i]) for i in range(2)
    ]
    fetch[0].start()
    for s in range(DEPTH):
        for copy in load(s):
            copy.start()
    for copy in fetch[1:]:
        copy.start()
    for s in range(len(steps)):
        i, j = steps[s]
        if s % NDP == 0:
            fetch[i].wait()
        for copy in load(s):
            copy.wait()
        if s >= 2:
            for copy in store(s - 2):
                copy.wait()
        for p in range(2):
            ready[s % 2, p] = jnp.dot(
                weights[i],
                rows[s % DEPTH, :, p * UNIT : (p + 1) * UNIT],
                preferred_element_type=jnp.float32,
            ).astype(jnp.bfloat16)
        for copy in store(s):
            copy.start()
        if s + DEPTH < len(steps):
            for copy in load(s + DEPTH):
                copy.start()
    for s in range(len(steps) - 2, len(steps)):
        for copy in store(s):
            copy.wait()


def partial(ring, where, weighted, buffers):
    any_spec = pl.BlockSpec(memory_space=pl.ANY)
    shapes = [(2, 2, H, UNIT)] * 3 + [(2, H, UNIT)] * 2 if ring else [(NDP, 2, 2, H, UNIT)]
    return pl.pallas_call(
        functools.partial(partial_kernel, ring),
        grid_spec=pltpu.PrefetchScalarGridSpec(
            num_scalar_prefetch=1,
            grid=(1,),
            in_specs=[any_spec] * (1 + len(buffers)),
            out_specs=[any_spec] * len(shapes),
            scratch_shapes=[
                pltpu.VMEM((2, H, SLOTS), jnp.bfloat16),
                pltpu.VMEM((DEPTH, SLOTS, HALF), jnp.bfloat16),
                pltpu.VMEM((2, 2, H, UNIT), jnp.bfloat16),
                pltpu.SemaphoreType.DMA((2,)),
                pltpu.SemaphoreType.DMA((DEPTH, 4)),
                pltpu.SemaphoreType.DMA((2, 2)),
            ],
        ),
        out_shape=[jax.ShapeDtypeStruct(shape, jnp.bfloat16) for shape in shapes],
        compiler_params=params(),
        cost_estimate=cost(
            2 * 2 * SLOTS * H * WIDE, 2 * (SLOTS * WIDE * 2 + H * WIDE * 2 + H * SLOTS * 2)
        ),
        name="partial",
    )(where, weighted, *buffers)


def grads_kernel(group, where_ref, factor_ref, effective_ref, *refs):
    buffers, refs = refs[:4], refs[4:]
    rows, eff, total, sems = refs[-4:]
    e = pl.program_id(0)

    def load(at, k):
        return [
            pltpu.make_async_copy(
                buffers[r].at[at, :, pl.ds(k * 1024, 1024)],
                rows.at[k, segment(where_ref, r)],
                sems.at[k, r],
            )
            for r in range(4)
        ] + [
            pltpu.make_async_copy(
                effective_ref.at[2 * k + j, group, at],
                eff.at[k, :, pl.ds(j * HALF, HALF)],
                sems.at[k, 4 + j],
            )
            for j in range(2)
        ]

    @pl.when(e == 0)
    def _():
        for k in range(2):
            for copy in load(0, k):
                copy.start()

    for k in range(2):
        for copy in load(e, k):
            copy.wait()
        for n in range(H // 256):
            columns = slice(n * 256, (n + 1) * 256)
            value = lax.dot_general(
                rows[k], eff[k, columns, :], (((1,), (1,)), ((), ())), preferred_element_type=jnp.float32
            )
            if k == 0:
                total[:, columns] = value
            else:
                total[:, columns] += value

        @pl.when(e == 0)
        def _(k=k):
            for copy in load(1, k):
                copy.start()

    def piece(i, carry):
        at = pl.ds(pl.multiple_of(i * 2 * PART, 2 * PART), 2 * PART)
        z = i // 2
        x = (i - z * 2) * 2
        source = [jnp.where(where_ref[4] == 0, (x + k) * NZ + z, 2 * i + k) for k in range(2)]
        product = jnp.concatenate(
            [total[pl.ds(pl.multiple_of(one * PART, PART), PART), :] for one in source], axis=0
        )
        if not group:
            refs[0][0, at, :] = product
            return carry
        before_ref, gate_ref, up_ref, weight_ref, gate_out, up_out, score_out = refs[:7]
        slot_grads = factor_ref[e] * (before_ref[0, at, :] + product)
        gate = gate_ref[0, at, :].astype(jnp.float32)
        up = up_ref[0, at, :].astype(jnp.float32)
        sig = 0.5 * jnp.tanh(0.5 * gate) + 0.5
        activated = gate * sig
        score_out[0, at, :] = jnp.sum(slot_grads * (activated * up), axis=1, keepdims=True)
        scaled = weight_ref[0, at, :] * slot_grads
        gate_out[0, at, :] = (scaled * up * (sig + activated * (1.0 - sig))).astype(jnp.bfloat16)
        up_out[0, at, :] = (scaled * activated).astype(jnp.bfloat16)
        return carry

    lax.fori_loop(0, SLOTS // (2 * PART), piece, 0)


def grads(group, where, factor, effective, buffers, others=()):
    any_spec = pl.BlockSpec(memory_space=pl.ANY)
    block = pl.BlockSpec((1, SLOTS, H), lambda n, s, f: (n, 0, 0))
    column = pl.BlockSpec((1, SLOTS, 1), lambda n, s, f: (n, 0, 0))
    shape = lambda dtype, width=H: jax.ShapeDtypeStruct((2, SLOTS, width), dtype)
    if group:
        ins, outs = [block, block, block, column], [block, block, column]
        shapes = [shape(jnp.bfloat16), shape(jnp.bfloat16), shape(jnp.float32, 1)]
    else:
        ins, outs, shapes = [], [block], [shape(jnp.float32)]
    return pl.pallas_call(
        functools.partial(grads_kernel, group),
        grid_spec=pltpu.PrefetchScalarGridSpec(
            num_scalar_prefetch=2,
            grid=(2,),
            in_specs=[any_spec] * 5 + ins,
            out_specs=outs,
            scratch_shapes=[
                pltpu.VMEM((2, SLOTS, 1024), jnp.bfloat16),
                pltpu.VMEM((2, H, 1024), jnp.bfloat16),
                pltpu.VMEM((SLOTS, H), jnp.float32),
                pltpu.SemaphoreType.DMA((2, 6)),
            ],
        ),
        out_shape=shapes,
        compiler_params=params(),
        cost_estimate=cost(
            2 * 2 * SLOTS * H * WIDE + group * 2 * SLOTS * H * 30,
            2 * (SLOTS * WIDE * 2 + H * WIDE * 2 + SLOTS * H * (12 if group else 4)),
        ),
        name=f"grads{group}",
    )(where, factor, effective, *buffers, *others)


def collect(own, up, down, low, high):
    wide = lambda value: value.astype(jnp.float32)
    return (
        wide(own[0, 0]) + (wide(low[0]) + wide(down[0, 0])),
        wide(own[1, 0]) + (wide(up[1, 0]) + wide(high[0])),
    )


PAIR = pl.BlockSpec((2, 1, H, UNIT), lambda n, *s: (0, n, 0, 0))
SINGLE = pl.BlockSpec((1, H, UNIT), lambda n, *s: (n, 0, 0))


def finish_kernel(where_ref, factor_ref, theirs, *refs):
    out_ref = refs[5]
    core = where_ref[4]
    factor = factor_ref[pl.program_id(0)]
    for p, value in enumerate(collect(*refs[:5])):
        mine = pl.ds(pl.multiple_of(core * HALF + p * UNIT, UNIT), UNIT)
        other = pl.ds(pl.multiple_of((1 - core) * HALF + p * UNIT, UNIT), UNIT)
        out_ref[0, :, mine] = (factor * value).astype(jnp.bfloat16)
        out_ref[0, :, other] = (factor * theirs[p, 0].astype(jnp.float32)).astype(jnp.bfloat16)


def finish(where, factor, theirs, pieces):
    return pl.pallas_call(
        finish_kernel,
        grid_spec=pltpu.PrefetchScalarGridSpec(
            num_scalar_prefetch=2,
            grid=(2,),
            in_specs=[PAIR] * 4 + [SINGLE] * 2,
            out_specs=pl.BlockSpec((1, H, 1024), lambda n, *s: (n, 0, 0)),
        ),
        out_shape=jax.ShapeDtypeStruct((2, H, 1024), jnp.bfloat16),
        compiler_params=params(),
        name="finish",
    )(where, factor, theirs, *pieces)


def after(value, *first):
    return lax.optimization_barrier((value, *first))[0]


def on_device(grad_out, expert_ids, route_weights, gate_values, up_values, w_down):
    me = lax.axis_index("expert")
    y = lax.axis_index("dp")
    core = me % 2
    x = (me // 2) % NX
    z = me // (2 * NX)
    move = lambda value, *to: lax.ppermute(value, "expert", pairs(*to))
    swap = lambda value: move(value, True, 0, 1)
    upward = lambda value: lax.ppermute(value, "dp", [(i, (i + 1) % NDP) for i in range(NDP)])
    downward = lambda value: lax.ppermute(value, "dp", [(i, (i - 1) % NDP) for i in range(NDP)])

    mine, theirs, share, rank = split(core, grad_out, expert_ids, route_weights)
    partner = swap(theirs)
    given, given_sums = shrink(1 - core, False, after(w_down, theirs))
    block = lax.dynamic_update_slice(mine, partner[None], (1 - core, 0, 0))
    block = after(block, given)
    blocks = [block, move(block, True, 1, 0), move(block, True, -1, 0)]
    blocks += [move(blocks[1][0], True, 1, 0), move(blocks[2][1], True, -1, 0)]
    kept, kept_sums = shrink(core, True, after(w_down, upward(given_sums)))
    effective = lax.dynamic_update_slice(kept, swap(given)[None], (0, 0, 0, 0))
    effective = lax.all_gather(effective, "dp", axis=0)

    share = share[:, :CAP].reshape(NZ * NX * 2, 2, CAP)
    share = lax.all_to_all(share, "expert", split_axis=0, concat_axis=0, tiled=True)
    sums = jnp.sum(given_sums + kept_sums, axis=(0, 3, 4))
    below, above = upward(sums), downward(sums)
    sums = (sums + upward(below)) + (below + above)
    factor = sums[:, 0] / (sums[:, 1] + epsilon)

    first, second = jnp.where(core == 0, z, x), jnp.where(core == 0, x, z)
    around = lambda value, sign: [(value + sign * shift) % 4 for shift in SHIFTS]
    held = jnp.stack([*around(first, -1), *around(second, 1), core, first]).astype(jnp.int32)
    where = jnp.stack([*around(second, -1), core, y]).astype(jnp.int32)
    gate, up = gate_values[0], up_values[0]

    def send(rows, before):
        return [rows[0]] + [
            move(after(rows[i], *before), False, SHIFTS[i], 0) for i in range(1, 4)
        ]

    rows = pick(1, after(held, factor, share), blocks)
    sent = send(rows, [])
    rows = pick(0, after(held, *rows), blocks)
    slot_weight = after(share, *rows).astype(jnp.float32).transpose(1, 0, 2).reshape(2, SLOTS, 1)
    weighted, their_weighted = weigh(core, gate, up, slot_weight)
    their_weighted = swap(after(their_weighted, *sent[1:]))

    def exchange(pieces):
        own, up_first, down_first, up_last, down_last = pieces
        return own, upward(up_first), downward(down_first), up_last, down_last

    def complete(pieces, *before):
        own, up_first, down_first, up_last, down_last = pieces
        up_last = upward(after(up_last, *before) + up_first[0])
        down_last = downward(after(down_last, *before) + down_first[1])
        return own, up_first, down_first, up_last, down_last

    own = send(rows, sent[1:])
    theirs = partial(False, where, their_weighted, sent)[0]
    before = grads(0, after(where, theirs), factor, effective, sent)[0]
    theirs = lax.psum_scatter(theirs, "dp", scatter_dimension=0, tiled=False)
    before = swap(after(before, *own[1:]))
    ours = exchange(partial(True, where, weighted, own))
    grad_gate, grad_up, scores = grads(
        1, where, factor, effective, own, (before, gate, up, slot_weight)
    )
    ours = complete(ours, scores)
    returned = lax.all_to_all(
        scores.reshape(2, SLOTS), "expert", split_axis=1, concat_axis=0, tiled=True
    )
    grad_route = back(expert_ids, rank, returned)
    summed = swap(theirs)
    grad_down = finish(where, factor, summed, ours)
    return (grad_gate[None], grad_up[None], grad_down, grad_route)


def solution(mesh):
    in_specs = (
        P(("dp", "expert"), None),
        P(("dp", "expert"), None),
        P(("dp", "expert"), None),
        P("dp", "expert", None, None),
        P("dp", "expert", None, None),
        P("expert", None, "dp"),
    )
    out_specs = (
        P("dp", "expert", None, None),
        P("dp", "expert", None, None),
        P("expert", None, "dp"),
        P(("dp", "expert"), None),
    )
    return jax.shard_map(
        on_device, mesh=mesh, in_specs=in_specs, out_specs=out_specs, check_vma=False
    )
```

profile of v0, /device:TPU:1, one launch (start us, length us, event | category | flops | bytes accessed | tf_op | source)
XLA Modules:
  0.0 310.0 jit_solution(1572337854404545658)
XLA Ops:
  7.2 1.3 convert_bitcast_fusion.1.weights_ref
  8.5 4.4 %split.1 = (bf16[2,272,2048]{2,1,0:T(8,128)(2,1)}, bf16[272,2048]{1,0:T(8,128)(2,1)}, bf16[64,128]{1,0:T(8,128)(2,1)}, f32[64,256]{1,0:T(8,128)}) custom-call(s32[1]{0:T(128)} %bitcast.4.core_ref.half_ref, bf16[256,4096]{1,0:T(8,128)(2,1)} %rows_ref.1, s32[8,256]{1,0:T(8,128)} %bitcast.54, f32[8,256]{1,0:T(8,128)} %convert_bitcast_fusion.1.weights_ref), custom_call_target="tpu_custom_call" | custom-call | tf_op jit(solution)/shard_map/split/pallas_call | solution.py:164
  12.9 4.9 %shrink.2 = (bf16[2,768,512]{2,1,0:T(8,128)(2,1)}, f32[2,2,2,8,128]{4,3,2,1,0:T(8,128)}) custom-call(s32[1]{0:T(128)} %bitcast.6.half_ref, bf16[2,768,1024]{2,1,0:T(8,128)(2,1)} %w_ref.1), custom_call_target="tpu_custom_call" | custom-call | flops 23592960 | bytes 3145728 | tf_op jit(solution)/shard_map/shrink/pallas_call | solution.py:86
  17.8 1.4 collective-permute-start.3
  19.2 4.9 %shrink.3 = (bf16[2,2,768,512]{3,2,1,0:T(8,128)(2,1)}, f32[2,2,2,8,128]{4,3,2,1,0:T(8,128)}) custom-call(s32[1]{0:T(128)} %bitcast.4.core_ref.half_ref, bf16[2,768,1024]{2,1,0:T(8,128)(2,1)} %w_ref.1), custom_call_target="tpu_custom_call" | custom-call | flops 23592960 | bytes 3145728 | tf_op jit(solution)/shard_map/shrink/pallas_call | solution.py:86
  24.1 1.2 bitcast_dynamic-update-slice_fusion
  25.5 2.9 collective-permute-done.4
  28.6 2.6 collective-permute-start.6
  31.3 24.4 %collective-permute-done.6.refs_2_ = bf16[2,272,2048]{2,1,0:T(8,128)(2,1)S(1)} collective-permute-done((bf16[2,272,2048]{2,1,0:T(8,128)(2,1)S(1)}, bf16[2,272,2048]{2,1,0:T(8,128)(2,1)S(1)}, u32[]{:S(2)}, u32[]{:S(2)}) %collective-permute-start.6) | collective-permute-done | bytes 2228256 | tf_op jit(solution)/shard_map/ppermute | solution.py:585
  55.7 3.6 %collective-permute-start.8 = (bf16[272,2048]{1,0:T(8,128)(2,1)S(1)}, bf16[272,2048]{1,0:T(8,128)(2,1)}, u32[]{:S(2)}, u32[]{:S(2)}) collective-permute-start(bf16[272,2048]{1,0:T(8,128)(2,1)S(1)} %slice_bitcast_fusion), channel_id=1, source_target_pairs={{0,24},{1,7},{2,26},{3,1},{4,28},{5,3},{6,30},{7,5},{8,0},{9,15},{... | collective-permute-start | bytes 3342344 | tf_op jit(solution)/shard_map/ppermute | solution.py:585
  59.5 1.1 copy-done.7
  60.8 2.8 collective-permute-start.2
  63.5 8.7 %all-to-all-start = ((bf16[32,2,36]{2,1,0:T(2,128)(2,1)}), bf16[32,2,36]{2,1,0:T(2,128)(2,1)S(1)}, u32[]{:S(2)}, u32[]{:S(2)}) async-start(bf16[32,2,36]{2,1,0:T(2,128)(2,1)} %bitcast.19), calls=%async_computation | async-start | bytes 32768 | tf_op jit(solution)/shard_map/all_to_all | solution.py:602
  73.4 4.0 %collective-permute-done.1 = f32[2,2]{1,0:T(2,128)S(1)} collective-permute-done((f32[2,2]{1,0:T(2,128)S(1)}, f32[2,2]{1,0:T(2,128)S(1)}, u32[]{:S(2)}, u32[]{:S(2)}) %collective-permute-start.1) | collective-permute-done | bytes 48 | tf_op jit(solution)/shard_map/ppermute | solution.py:587
  78.1 1.1 all-to-all-done
  79.2 1.0 copy-done.12
  80.2 9.9 %pick0.1 = (bf16[2,288,2048]{2,1,0:T(8,128)(2,1)}, bf16[2,288,2048]{2,1,0:T(8,128)(2,1)}, bf16[2,288,2048]{2,1,0:T(8,128)(2,1)}, bf16[2,288,2048]{2,1,0:T(8,128)(2,1)}) custom-call(s32[10]{0:T(128)} %stack.65.where_ref, bf16[2,272,2048]{2,1,0:T(8,128)(2,1)} %copy-done.11, bf16[2,272,2048]{2,1,0:T(8,128)(2,1)} %copy-done.7, bf16[2,272,2048]{2,1,0:T(8,128)(2,1)} %copy-done.6, ...), custom_call_target="tpu_custom_call" | custom-call | flops 4831838208 | bytes 17825792 | tf_op jit(solution)/shard_map/pick0/pallas_call | solution.py:259
  90.1 1.9 collective-permute-start.11
  92.0 0.9 collective-permute-start.10
  93.5 9.9 %pick1.1 = (bf16[2,288,2048]{2,1,0:T(8,128)(2,1)}, bf16[2,288,2048]{2,1,0:T(8,128)(2,1)}, bf16[2,288,2048]{2,1,0:T(8,128)(2,1)}, bf16[2,288,2048]{2,1,0:T(8,128)(2,1)}) custom-call(s32[10]{0:T(128)} %stack.65.where_ref, bf16[2,272,2048]{2,1,0:T(8,128)(2,1)} %copy-done.11, bf16[2,272,2048]{2,1,0:T(8,128)(2,1)} %copy-done.7, bf16[2,272,2048]{2,1,0:T(8,128)(2,1)} %copy-done.6, ...), custom_call_target="tpu_custom_call" | custom-call | flops 4831838208 | bytes 17825792 | tf_op jit(solution)/shard_map/pick1/pallas_call | solution.py:259
  103.5 1.4 reshape.40.weight_ref.refs_7_
  104.8 9.3 %weigh.1 = (bf16[2,768,1152]{2,1,0:T(8,128)(2,1)}, bf16[2,768,1152]{2,1,0:T(8,128)(2,1)}) custom-call(s32[1]{0:T(128)} %bitcast.4.core_ref.half_ref, bf16[2,1152,768]{2,1,0:T(8,128)(2,1)} %bitcast.48, bf16[2,1152,768]{2,1,0:T(8,128)(2,1)} %bitcast.50, f32[2,1152,1]{2,1,0:T(8,128)} %reshape.40.weight_ref.refs_7_), custom_call_target="tpu_custom_call" | custom-call | flops 35389440 | bytes 14155776 | tf_op jit(solution)/shard_map/weigh/pallas_call | solution.py:312
  114.1 5.8 %collective-permute-done.11.refs_3_ = bf16[2,288,2048]{2,1,0:T(8,128)(2,1)S(1)} collective-permute-done((bf16[2,288,2048]{2,1,0:T(8,128)(2,1)}, bf16[2,288,2048]{2,1,0:T(8,128)(2,1)S(1)}, u32[]{:S(2)}, u32[]{:S(2)}) %collective-permute-start.11) | collective-permute-done | bytes 2359328 | tf_op jit(solution)/shard_map/ppermute | solution.py:585
  119.9 24.6 %collective-permute-done.10.refs_2_ = bf16[2,288,2048]{2,1,0:T(8,128)(2,1)} collective-permute-done((bf16[2,288,2048]{2,1,0:T(8,128)(2,1)}, bf16[2,288,2048]{2,1,0:T(8,128)(2,1)}, u32[]{:S(2)}, u32[]{:S(2)}) %collective-permute-start.10) | collective-permute-done | bytes 2359328 | tf_op jit(solution)/shard_map/ppermute | solution.py:585
  144.5 0.8 collective-permute-done.9.refs_1_
  145.3 1.5 collective-permute-start.15
  147.4 5.6 %collective-permute-done.15.weighted_ref = bf16[2,768,1152]{2,1,0:T(8,128)(2,1)} collective-permute-done((bf16[2,768,1152]{2,1,0:T(8,128)(2,1)}, bf16[2,768,1152]{2,1,0:T(8,128)(2,1)}, u32[]{:S(2)}, u32[]{:S(2)}) %collective-permute-start.15) | collective-permute-done | bytes 3538976 | tf_op jit(solution)/shard_map/ppermute | solution.py:585
  153.0 13.6 %partial.2 = bf16[4,2,2,768,256]{4,3,2,1,0:T(8,128)(2,1)} custom-call(s32[6]{0:T(128)} %stack.56.where_ref, bf16[2,768,1152]{2,1,0:T(8,128)(2,1)} %collective-permute-done.15.weighted_ref, bf16[2,288,2048]{2,1,0:T(8,128)(2,1)} %get-tuple-element.53.refs_0_, bf16[2,288,2048]{2,1,0:T(8,128)(2,1)} %collective-permute-done.9.refs_1_, ...), custom_call_target="tpu_custom_call" | custom-call | flops 7247757312 | bytes 19267584 | tf_op jit(solution)/shard_map/partial/pallas_call | solution.py:406
  167.3 2.1 collective-permute-start.13
  169.4 0.9 collective-permute-start.14
  170.2 16.0 %grads0.1 = f32[2,1152,768]{2,1,0:T(8,128)} custom-call(s32[6]{0:T(128)} %stack.56.where_ref, f32[2]{0:T(128)} %fusion.2.factor_ref, bf16[4,2,2,768,512]{4,3,2,1,0:T(8,128)(2,1)} %all-gather.2.cloned.1.call-done.effective_ref, bf16[2,288,2048]{2,1,0:T(8,128)(2,1)} %get-tuple-element.53.refs_0_, bf16[2,288,2048]{2,1,0:T(8,128)(2,1)} %collective-permute-done.9.refs_1_, ...), custom_call_target="tpu_custom_call" | custom-call | flops 7247757312 | bytes 22806528 | tf_op jit(solution)/shard_map/grads0/pallas_call | solution.py:513
  186.2 10.0 %collective-permute-done.12.refs_1_ = bf16[2,288,2048]{2,1,0:T(8,128)(2,1)S(1)} collective-permute-done((bf16[2,288,2048]{2,1,0:T(8,128)(2,1)}, bf16[2,288,2048]{2,1,0:T(8,128)(2,1)S(1)}, u32[]{:S(2)}, u32[]{:S(2)}) %collective-permute-start.12) | collective-permute-done | bytes 2359328 | tf_op jit(solution)/shard_map/ppermute | solution.py:585
  196.2 24.6 %collective-permute-done.13.refs_2_ = bf16[2,288,2048]{2,1,0:T(8,128)(2,1)} collective-permute-done((bf16[2,288,2048]{2,1,0:T(8,128)(2,1)}, bf16[2,288,2048]{2,1,0:T(8,128)(2,1)}, u32[]{:S(2)}, u32[]{:S(2)}) %collective-permute-start.13) | collective-permute-done | bytes 2359328 | tf_op jit(solution)/shard_map/ppermute | solution.py:585
  220.8 1.1 collective-permute-done.14.refs_3_
  221.8 1.1 collective-permute-start.16
  222.9 13.8 %partial.3 = (bf16[2,2,768,256]{3,2,1,0:T(8,128)(2,1)}, bf16[2,2,768,256]{3,2,1,0:T(8,128)(2,1)}, bf16[2,2,768,256]{3,2,1,0:T(8,128)(2,1)}, bf16[2,768,256]{2,1,0:T(8,128)(2,1)}, bf16[2,768,256]{2,1,0:T(8,128)(2,1)}) custom-call(s32[6]{0:T(128)} %stack.56.where_ref, bf16[2,768,1152]{2,1,0:T(8,128)(2,1)} %get-tuple-element.72.weighted_ref, ...), custom_call_target="tpu_custom_call" | custom-call | flops 7247757312 | bytes 19267584 | tf_op jit(solution)/shard_map/partial/pallas_call | solution.py:406
  236.8 1.2 collective-permute-start.18
  238.0 1.8 collective-permute-start.19
  239.7 1.4 collective-permute-start.17
  241.1 26.3 %grads1.1 = (bf16[2,1152,768]{2,1,0:T(8,128)(2,1)}, bf16[2,1152,768]{2,1,0:T(8,128)(2,1)}, f32[2,1152,1]{2,1,0:T(8,128)}) custom-call(s32[6]{0:T(128)} %stack.56.where_ref, f32[2]{0:T(128)} %fusion.2.factor_ref, bf16[4,2,2,768,512]{4,3,2,1,0:T(8,128)(2,1)} %all-gather.2.cloned.1.call-done.effective_ref, bf16[2,288,2048]{2,1,0:T(8,128)(2,1)} %get-tuple-element.58.refs_0_, ...), custom_call_target="tpu_custom_call" | custom-call | flops 7300841472 | bytes 36962304 | tf_op jit(solution)/shard_map/grads1/pallas_call | solution.py:513
  267.4 6.1 %collective-permute-done.18.refs_1_ = bf16[2,2,768,256]{3,2,1,0:T(8,128)(2,1)S(1)} collective-permute-done((bf16[2,2,768,256]{3,2,1,0:T(8,128)(2,1)}, bf16[2,2,768,256]{3,2,1,0:T(8,128)(2,1)S(1)}, u32[]{:S(2)}, u32[]{:S(2)}) %collective-permute-start.18) | collective-permute-done | bytes 1572896 | tf_op jit(solution)/shard_map/ppermute | solution.py:587
  273.5 1.1 fusion.1
  275.3 1.1 fusion
  276.3 2.0 collective-permute-start.21
  278.3 1.6 reduce.1
  280.1 15.5 %all_to_all.24 = f32[2,32,36]{2,0,1:T(2,128)} all-to-all(f32[2,32,36]{2,0,1:T(2,128)S(1)} %copy.23), channel_id=1, replica_groups=mesh['dp'=4,'expert'=32] {'expert'}, dimensions={1} | all-to-all | bytes 18432 | tf_op jit(solution)/shard_map/all_to_all | solution.py:646
  295.6 2.0 back.1
  297.6 5.5 %finish.1 = bf16[2,768,1024]{2,1,0:T(8,128)(2,1)} custom-call(s32[6]{0:T(128)} %stack.56.where_ref, f32[2]{0:T(128)} %fusion.2.factor_ref, bf16[2,2,768,256]{3,2,1,0:T(8,128)(2,1)} %collective-permute-done.17.theirs, bf16[2,2,768,256]{3,2,1,0:T(8,128)(2,1)} %get-tuple-element.73.refs_0_, bf16[2,2,768,256]{3,2,1,0:T(8,128)(2,1)} %copy-done, ...), custom_call_target="tpu_custom_call" | custom-call | tf_op jit(solution)/shard_map/finish/pallas_call | solution.py:561
  (61 shorter events, 5.1 us)
Async XLA Ops:
  7.2 163.1 %all-gather.2.cloned.1.call-start = ((), (), s32[]{:S(2)}) async-start(), calls=%async_computation.3 | async-start | bytes 15728640 | tf_op jit(solution)/shard_map/all_gather | solution.py:599
  17.8 6.3 %collective-permute-start.3 = (bf16[2,768,512]{2,1,0:T(8,128)(2,1)}, bf16[2,768,512]{2,1,0:T(8,128)(2,1)S(1)}, u32[]{:S(2)}, u32[]{:S(2)}) collective-permute-start(bf16[2,768,512]{2,1,0:T(8,128)(2,1)} %get-tuple-element.48), channel_id=1, source_target_pairs={{0,1},{1,0},{2,3},{3,2},{4,5},{5,4},{6,7},{7,6},{8,9},{9,8},{10,11... | collective-permute-start | bytes 4718600 | tf_op jit(solution)/shard_map/ppermute | solution.py:585
  25.4 3.1 copy-start.10
  25.4 3.0 collective-permute-start.4
  28.6 30.7 %copy-start.11 = (bf16[2,272,2048]{2,1,0:T(8,128)(2,1)}, bf16[2,272,2048]{2,1,0:T(8,128)(2,1)S(1)}, u32[]{:S(2)}) copy-start(bf16[2,272,2048]{2,1,0:T(8,128)(2,1)S(1)} %bitcast_dynamic-update-slice_fusion.1.refs_0_) | copy-start | bytes 6684676
  28.6 32.1 %copy-start.8 = (f32[2,2,2,8,128]{4,3,2,1,0:T(8,128)S(1)}, f32[2,2,2,8,128]{4,3,2,1,0:T(8,128)}, u32[]{:S(2)}) copy-start(f32[2,2,2,8,128]{4,3,2,1,0:T(8,128)} %get-tuple-element.45) | copy-start | bytes 98308
  28.6 32.1 %copy-start.9 = (f32[2,2,2,8,128]{4,3,2,1,0:T(8,128)S(1)}, f32[2,2,2,8,128]{4,3,2,1,0:T(8,128)}, u32[]{:S(2)}) copy-start(f32[2,2,2,8,128]{4,3,2,1,0:T(8,128)} %get-tuple-element.46) | copy-start | bytes 98308
  28.6 27.0 %collective-permute-start.6 = (bf16[2,272,2048]{2,1,0:T(8,128)(2,1)S(1)}, bf16[2,272,2048]{2,1,0:T(8,128)(2,1)S(1)}, u32[]{:S(2)}, u32[]{:S(2)}) collective-permute-start(bf16[2,272,2048]{2,1,0:T(8,128)(2,1)S(1)} %bitcast_dynamic-update-slice_fusion.1.refs_0_), channel_id=1, source_target_pairs={{0,24},{1,7},{2,26},{3,1},{4,28},{5,3},{6,30},{7,5},{8,0},{9,15},{... | collective-permute-start | bytes 6684680 | tf_op jit(solution)/shard_map/ppermute | solution.py:585
  31.3 28.1 %collective-permute-start.5 = (bf16[2,272,2048]{2,1,0:T(8,128)(2,1)S(1)}, bf16[2,272,2048]{2,1,0:T(8,128)(2,1)S(1)}, u32[]{:S(2)}, u32[]{:S(2)}) collective-permute-start(bf16[2,272,2048]{2,1,0:T(8,128)(2,1)S(1)} %bitcast_dynamic-update-slice_fusion.1.refs_0_), channel_id=1, source_target_pairs={{0,8},{1,3},{2,10},{3,5},{4,12},{5,7},{6,14},{7,1},{8,16},{9,11},{... | collective-permute-start | bytes 6684680 | tf_op jit(solution)/shard_map/ppermute | solution.py:585
  55.6 3.8 %copy-start.6 = (bf16[2,272,2048]{2,1,0:T(8,128)(2,1)}, bf16[2,272,2048]{2,1,0:T(8,128)(2,1)S(1)}, u32[]{:S(2)}) copy-start(bf16[2,272,2048]{2,1,0:T(8,128)(2,1)S(1)} %collective-permute-done.6.refs_2_) | copy-start | bytes 6684676
  55.7 23.5 %collective-permute-start.8 = (bf16[272,2048]{1,0:T(8,128)(2,1)S(1)}, bf16[272,2048]{1,0:T(8,128)(2,1)}, u32[]{:S(2)}, u32[]{:S(2)}) collective-permute-start(bf16[272,2048]{1,0:T(8,128)(2,1)S(1)} %slice_bitcast_fusion), channel_id=1, source_target_pairs={{0,24},{1,7},{2,26},{3,1},{4,28},{5,3},{6,30},{7,5},{8,0},{9,15},{... | collective-permute-start | bytes 3342344 | tf_op jit(solution)/shard_map/ppermute | solution.py:585
  59.3 1.4 copy-start.7
  59.4 19.7 %collective-permute-start.7 = (bf16[272,2048]{1,0:T(8,128)(2,1)S(1)}, bf16[272,2048]{1,0:T(8,128)(2,1)S(1)}, u32[]{:S(2)}, u32[]{:S(2)}) collective-permute-start(bf16[272,2048]{1,0:T(8,128)(2,1)S(1)} %slice_bitcast_fusion.1), channel_id=1, source_target_pairs={{0,8},{1,3},{2,10},{3,5},{4,12},{5,7},{6,14},{7,1},{8,16},{9,11},{... | collective-permute-start | bytes 3342344 | tf_op jit(solution)/shard_map/ppermute | solution.py:585
  60.8 12.6 %collective-permute-start.2 = (f32[2,2]{1,0:T(2,128)S(1)}, f32[2,2]{1,0:T(2,128)S(1)}, u32[]{:S(2)}, u32[]{:S(2)}) collective-permute-start(f32[2,2]{1,0:T(2,128)S(1)} %add_reduce_fusion), channel_id=1, source_target_pairs={{0,96},{32,0},{64,32},{96,64},{1,97},{33,1},{65,33},{97,65},{2,98}... | collective-permute-start | bytes 56 | tf_op jit(solution)/shard_map/ppermute | solution.py:588
  63.5 9.5 %collective-permute-start = (f32[2,2]{1,0:T(2,128)S(1)}, f32[2,2]{1,0:T(2,128)S(1)}, u32[]{:S(2)}, u32[]{:S(2)}) collective-permute-start(f32[2,2]{1,0:T(2,128)S(1)} %add_reduce_fusion), channel_id=1, source_target_pairs={{0,32},{32,64},{64,96},{96,0},{1,33},{33,65},{65,97},{97,1},{2,34}... | collective-permute-start | bytes 56 | tf_op jit(solution)/shard_map/ppermute | solution.py:587
  63.5 15.6 %all-to-all-start = ((bf16[32,2,36]{2,1,0:T(2,128)(2,1)}), bf16[32,2,36]{2,1,0:T(2,128)(2,1)S(1)}, u32[]{:S(2)}, u32[]{:S(2)}) async-start(bf16[32,2,36]{2,1,0:T(2,128)(2,1)} %bitcast.19), calls=%async_computation | async-start | bytes 32768 | tf_op jit(solution)/shard_map/all_to_all | solution.py:602
  72.2 167.5 %reduce-scatter.2.cloned.1.call-start = ((), (), s32[]{:S(2)}) async-start(), calls=%async_computation.4 | async-start | bytes 7864320 | tf_op jit(solution)/shard_map/reduce_scatter | solution.py:639
  73.1 4.3 %collective-permute-start.1 = (f32[2,2]{1,0:T(2,128)S(1)}, f32[2,2]{1,0:T(2,128)S(1)}, u32[]{:S(2)}, u32[]{:S(2)}) collective-permute-start(f32[2,2]{1,0:T(2,128)S(1)} %collective-permute-done), channel_id=1, source_target_pairs={{0,32},{32,64},{64,96},{96,0},{1,33},{33,65},{65,97},{97,1},{2,34}... | collective-permute-start | bytes 56 | tf_op jit(solution)/shard_map/ppermute | solution.py:587
  79.2 1.0 copy-start.12
  90.1 29.8 %collective-permute-start.11 = (bf16[2,288,2048]{2,1,0:T(8,128)(2,1)}, bf16[2,288,2048]{2,1,0:T(8,128)(2,1)S(1)}, u32[]{:S(2)}, u32[]{:S(2)}) collective-permute-start(bf16[2,288,2048]{2,1,0:T(8,128)(2,1)} %get-tuple-element.56), channel_id=1, source_target_pairs={{0,4},{1,17},{2,6},{3,19},{4,0},{5,21},{6,2},{7,23},{8,12},{9,25},... | collective-permute-start | bytes 7077896 | tf_op jit(solution)/shard_map/ppermute | solution.py:585
  92.0 52.5 %collective-permute-start.10 = (bf16[2,288,2048]{2,1,0:T(8,128)(2,1)}, bf16[2,288,2048]{2,1,0:T(8,128)(2,1)}, u32[]{:S(2)}, u32[]{:S(2)}) collective-permute-start(bf16[2,288,2048]{2,1,0:T(8,128)(2,1)} %get-tuple-element.55), channel_id=1, source_target_pairs={{0,6},{1,25},{2,0},{3,27},{4,2},{5,29},{6,4},{7,31},{8,14},{9,1},{... | collective-permute-start | bytes 7077896 | tf_op jit(solution)/shard_map/ppermute | solution.py:585
  92.9 52.4 %collective-permute-start.9 = (bf16[2,288,2048]{2,1,0:T(8,128)(2,1)}, bf16[2,288,2048]{2,1,0:T(8,128)(2,1)}, u32[]{:S(2)}, u32[]{:S(2)}) collective-permute-start(bf16[2,288,2048]{2,1,0:T(8,128)(2,1)} %get-tuple-element.54), channel_id=1, source_target_pairs={{0,2},{1,9},{2,4},{3,11},{4,6},{5,13},{6,0},{7,15},{8,10},{9,17},{... | collective-permute-start | bytes 7077896 | tf_op jit(solution)/shard_map/ppermute | solution.py:585
  119.9 33.0 %copy-start.2 = (bf16[2,288,2048]{2,1,0:T(8,128)(2,1)}, bf16[2,288,2048]{2,1,0:T(8,128)(2,1)S(1)}, u32[]{:S(2)}) copy-start(bf16[2,288,2048]{2,1,0:T(8,128)(2,1)S(1)} %collective-permute-done.11.refs_3_) | copy-start | bytes 7077892
  145.3 7.7 %collective-permute-start.15 = (bf16[2,768,1152]{2,1,0:T(8,128)(2,1)}, bf16[2,768,1152]{2,1,0:T(8,128)(2,1)}, u32[]{:S(2)}, u32[]{:S(2)}) collective-permute-start(bf16[2,768,1152]{2,1,0:T(8,128)(2,1)} %get-tuple-element.67), channel_id=1, source_target_pairs={{0,1},{1,0},{2,3},{3,2},{4,5},{5,4},{6,7},{7,6},{8,9},{9,8},{10,11... | collective-permute-start | bytes 10616840 | tf_op jit(solution)/shard_map/ppermute | solution.py:585
  166.6 29.6 %collective-permute-start.12 = (bf16[2,288,2048]{2,1,0:T(8,128)(2,1)}, bf16[2,288,2048]{2,1,0:T(8,128)(2,1)S(1)}, u32[]{:S(2)}, u32[]{:S(2)}) collective-permute-start(bf16[2,288,2048]{2,1,0:T(8,128)(2,1)} %get-tuple-element.60), channel_id=1, source_target_pairs={{0,2},{1,9},{2,4},{3,11},{4,6},{5,13},{6,0},{7,15},{8,10},{9,17},{... | collective-permute-start | bytes 7077896 | tf_op jit(solution)/shard_map/ppermute | solution.py:585
  167.3 53.5 %collective-permute-start.13 = (bf16[2,288,2048]{2,1,0:T(8,128)(2,1)}, bf16[2,288,2048]{2,1,0:T(8,128)(2,1)}, u32[]{:S(2)}, u32[]{:S(2)}) collective-permute-start(bf16[2,288,2048]{2,1,0:T(8,128)(2,1)} %get-tuple-element.62), channel_id=1, source_target_pairs={{0,6},{1,25},{2,0},{3,27},{4,2},{5,29},{6,4},{7,31},{8,14},{9,1},{... | collective-permute-start | bytes 7077896 | tf_op jit(solution)/shard_map/ppermute | solution.py:585
  169.4 52.5 %collective-permute-start.14 = (bf16[2,288,2048]{2,1,0:T(8,128)(2,1)}, bf16[2,288,2048]{2,1,0:T(8,128)(2,1)}, u32[]{:S(2)}, u32[]{:S(2)}) collective-permute-start(bf16[2,288,2048]{2,1,0:T(8,128)(2,1)} %get-tuple-element.64), channel_id=1, source_target_pairs={{0,4},{1,17},{2,6},{3,19},{4,0},{5,21},{6,2},{7,23},{8,12},{9,25},... | collective-permute-start | bytes 7077896 | tf_op jit(solution)/shard_map/ppermute | solution.py:585
  196.2 26.7 %copy-start.3 = (bf16[2,288,2048]{2,1,0:T(8,128)(2,1)}, bf16[2,288,2048]{2,1,0:T(8,128)(2,1)S(1)}, u32[]{:S(2)}) copy-start(bf16[2,288,2048]{2,1,0:T(8,128)(2,1)S(1)} %collective-permute-done.12.refs_1_) | copy-start | bytes 7077892
  221.8 19.3 %collective-permute-start.16 = (f32[2,1152,768]{2,1,0:T(8,128)}, f32[2,1152,768]{2,1,0:T(8,128)}, u32[]{:S(2)}, u32[]{:S(2)}) collective-permute-start(f32[2,1152,768]{2,1,0:T(8,128)} %grads0.1), channel_id=1, source_target_pairs={{0,1},{1,0},{2,3},{3,2},{4,5},{5,4},{6,7},{7,6},{8,9},{9,8},{10,11... | collective-permute-start | bytes 21233672 | tf_op jit(solution)/shard_map/ppermute | solution.py:585
  236.8 36.7 %collective-permute-start.18 = (bf16[2,2,768,256]{3,2,1,0:T(8,128)(2,1)}, bf16[2,2,768,256]{3,2,1,0:T(8,128)(2,1)S(1)}, u32[]{:S(2)}, u32[]{:S(2)}) collective-permute-start(bf16[2,2,768,256]{3,2,1,0:T(8,128)(2,1)} %get-tuple-element.74), channel_id=1, source_target_pairs={{0,32},{32,64},{64,96},{96,0},{1,33},{33,65},{65,97},{97,1},{2,34}... | collective-permute-start | bytes 4718600 | tf_op jit(solution)/shard_map/ppermute | solution.py:587
  238.0 37.3 %collective-permute-start.19 = (bf16[2,2,768,256]{3,2,1,0:T(8,128)(2,1)}, bf16[2,2,768,256]{3,2,1,0:T(8,128)(2,1)S(1)}, u32[]{:S(2)}, u32[]{:S(2)}) collective-permute-start(bf16[2,2,768,256]{3,2,1,0:T(8,128)(2,1)} %get-tuple-element.75), channel_id=1, source_target_pairs={{0,96},{32,0},{64,32},{96,64},{1,97},{33,1},{65,33},{97,65},{2,98}... | collective-permute-start | bytes 4718600 | tf_op jit(solution)/shard_map/ppermute | solution.py:588
  239.7 33.8 %copy-start.5 = (bf16[2,768,256]{2,1,0:T(8,128)(2,1)S(1)}, bf16[2,768,256]{2,1,0:T(8,128)(2,1)}, u32[]{:S(2)}) copy-start(bf16[2,768,256]{2,1,0:T(8,128)(2,1)} %get-tuple-element.78) | copy-start | bytes 2359300
  239.7 57.9 %collective-permute-start.17 = (bf16[2,2,768,256]{3,2,1,0:T(8,128)(2,1)}, bf16[2,2,768,256]{3,2,1,0:T(8,128)(2,1)}, u32[]{:S(2)}, u32[]{:S(2)}) collective-permute-start(bf16[2,2,768,256]{3,2,1,0:T(8,128)(2,1)} %bitcast.59), channel_id=1, source_target_pairs={{0,1},{1,0},{2,3},{3,2},{4,5},{5,4},{6,7},{7,6},{8,9},{9,8},{10,11... | collective-permute-start | bytes 4718600 | tf_op jit(solution)/shard_map/ppermute | solution.py:585
  267.4 7.9 %copy-start.4 = (bf16[2,768,256]{2,1,0:T(8,128)(2,1)S(1)}, bf16[2,768,256]{2,1,0:T(8,128)(2,1)}, u32[]{:S(2)}) copy-start(bf16[2,768,256]{2,1,0:T(8,128)(2,1)} %get-tuple-element.80) | copy-start | bytes 2359300
  273.5 2.8 copy-start
  274.6 23.0 %collective-permute-start.20 = (bf16[2,768,256]{2,1,0:T(8,128)(2,1)}, bf16[2,768,256]{2,1,0:T(8,128)(2,1)}, u32[]{:S(2)}, u32[]{:S(2)}) collective-permute-start(bf16[2,768,256]{2,1,0:T(8,128)(2,1)} %fusion.1), channel_id=1, source_target_pairs={{0,32},{32,64},{64,96},{96,0},{1,33},{33,65},{65,97},{97,1},{2,34}... | collective-permute-start | bytes 2359304 | tf_op jit(solution)/shard_map/ppermute | solution.py:587
  275.3 22.3 %copy-start.1 = (bf16[2,2,768,256]{3,2,1,0:T(8,128)(2,1)}, bf16[2,2,768,256]{3,2,1,0:T(8,128)(2,1)S(1)}, u32[]{:S(2)}) copy-start(bf16[2,2,768,256]{3,2,1,0:T(8,128)(2,1)S(1)} %collective-permute-done.19.refs_2_) | copy-start | bytes 4718596
  276.3 21.3 %collective-permute-start.21 = (bf16[2,768,256]{2,1,0:T(8,128)(2,1)}, bf16[2,768,256]{2,1,0:T(8,128)(2,1)}, u32[]{:S(2)}, u32[]{:S(2)}) collective-permute-start(bf16[2,768,256]{2,1,0:T(8,128)(2,1)} %fusion), channel_id=1, source_target_pairs={{0,96},{32,0},{64,32},{96,64},{1,97},{33,1},{65,33},{97,65},{2,98}... | collective-permute-start | bytes 2359304 | tf_op jit(solution)/shard_map/ppermute | solution.py:588
Sparse Core Ops, SparseCore 0:
  25.5 120.5 all-gather.1
  166.7 63.1 reduce-scatter.1
where the time goes:
time: 311 us; the launch traced here: 310 us
  Pallas kernels  121 us (39%)
  waiting for transfers between devices  111 us (36%)
  starting transfers between devices  36.3 us (12%)
  blocking collectives  15.5 us (5%)
  between operations  14.4 us (5%)
  local copies, waits for them, and re-layouts  6.5 us (2%)
  other arithmetic  5.91 us (2%)
    ppermute x15, waiting for transfers between devices, on_device(): move = lambda value, *to: lax.ppermute(value, 'expert', pairs(*to))  99.7 us
    pallas_call x2, Pallas kernels, grads(): pl.pallas_call(functools.partial(grads_kernel, group), grid_spec=pltpu.Pr...  42.3 us
    pallas_call x2, Pallas kernels, partial(): pl.pallas_call(functools.partial(partial_kernel, ring), grid_spec=pltpu.P...  27.4 us
    pallas_call x2, Pallas kernels, pick(): pl.pallas_call(functools.partial(pick_kernel, swap), grid_spec=pltpu.Pref...  19.8 us
    ppermute x15, starting transfers between devices, on_device(): move = lambda value, *to: lax.ppermute(value, 'expert', pairs(*to))  18.8 us
    all_to_all x1, blocking collectives, on_device(): lax.all_to_all(scores.reshape(2, SLOTS), 'expert', split_axis=1, concat_a...  15.5 us
    ppermute x4, waiting for transfers between devices, on_device(): lax.ppermute(value, 'dp', [(i, (i + 1) % NDP) for i in range(NDP)])  10.1 us
    pallas_call x2, Pallas kernels, shrink(): pl.pallas_call(shrink_kernel, grid_spec=pltpu.PrefetchScalarGridSpec(num_...  9.82 us
  transfers between devices with their start and end apart: 25, of which 12 were waited for; matrix products, arithmetic and copies ran while one was open for 2% of the time, Pallas kernels for 34%

commit v1 on v0

--- a/solution.py
+++ b/solution.py
@@ -185,9 +185,13 @@
     )(core.reshape(1).astype(jnp.int32), rows, ids.T, weights.astype(jnp.float32).T)
 
 
+def held_by(buffers, to, e):
+    return buffers[2 * to - 1 + e] if to in (1, 2) else buffers[min(to * 2, 5)].at[e]
+
+
 def pick_kernel(swap, where_ref, *refs):
-    outs = refs[5:9]
-    tokens, coded, ranks, onehot, picked, sems = refs[9:]
+    outs = refs[5:11]
+    tokens, coded, ranks, onehot, picked, sems = refs[11:]
     blocks = [[ref.at[part] for part in range(2)] for ref in refs[:3]] + [refs[3:5]]
     step = pl.program_id(0)
     core = where_ref[8]
@@ -251,10 +255,12 @@
     for i in range(8):
         rows = pl.ds(i * PART, PART)
         joined = jnp.concatenate([picked[block, rows, :] for block in range(4)], axis=0)
-        outs[i // 2][i % 2] = joined.astype(jnp.bfloat16)
+        held_by(outs, i // 2, i % 2)[...] = joined.astype(jnp.bfloat16)
 
 
 def pick(swap, where, blocks):
+    pair = pl.BlockSpec((2, SEG, HALF), lambda n, s: (0, 0, n))
+    single = pl.BlockSpec((SEG, HALF), lambda n, s: (0, n))
     any_spec = pl.BlockSpec(memory_space=pl.ANY)
     return pl.pallas_call(
         functools.partial(pick_kernel, swap),
@@ -262,7 +268,7 @@
             num_scalar_prefetch=1,
             grid=(4,),
             in_specs=[any_spec] * 5,
-            out_specs=[pl.BlockSpec((2, SEG, HALF), lambda n, s: (0, 0, n))] * 4,
+            out_specs=[pair] + [single] * 4 + [pair],
             scratch_shapes=[
                 pltpu.VMEM((4, 4, 2 * TOK, HALF), jnp.bfloat16),
                 pltpu.VMEM((4, 2, 16, WIDE), jnp.bfloat16),
@@ -272,7 +278,9 @@
                 pltpu.SemaphoreType.DMA((5, 8)),
             ],
         ),
-        out_shape=[jax.ShapeDtypeStruct((2, SEG, WIDE), jnp.bfloat16)] * 4,
+        out_shape=[
+            jax.ShapeDtypeStruct((2, SEG, WIDE) if n in (0, 5) else (SEG, WIDE), jnp.bfloat16) for n in range(6)
+        ],
         compiler_params=params(),
         cost_estimate=cost(2 * 4 * 576 * 512 * WIDE, 8 * TOK * WIDE * 2 + 8 * SEG * WIDE * 2),
         name=f"pick{1 - swap}",
@@ -333,7 +341,7 @@
 
 
 def partial_kernel(ring, where_ref, weighted_ref, *refs):
-    buffers, outs = refs[:4], refs[4:-6]
+    buffers, outs = refs[:6], refs[6:-6]
     weights, rows, ready, weight_sems, in_sems, out_sems = refs[-6:]
     steps = [(i, j) for i in range(2) for j in (3, 1, 2, 0)]
 
@@ -343,7 +351,7 @@
         columns = pl.ds(pl.multiple_of(at * HALF, HALF), HALF)
         return [
             pltpu.make_async_copy(
-                buffers[r].at[i, :, columns],
+                held_by(buffers, r, i).at[:, columns],
                 rows.at[s % DEPTH, segment(where_ref, r)],
                 in_sems.at[s % DEPTH, r],
             )
@@ -429,14 +437,14 @@
 
 
 def grads_kernel(group, where_ref, factor_ref, effective_ref, *refs):
-    buffers, refs = refs[:4], refs[4:]
+    buffers, refs = refs[:6], refs[6:]
     rows, eff, total, sems = refs[-4:]
     e = pl.program_id(0)
 
     def load(at, k):
         return [
             pltpu.make_async_copy(
-                buffers[r].at[at, :, pl.ds(k * 1024, 1024)],
+                held_by(buffers, r, at).at[:, pl.ds(k * 1024, 1024)],
                 rows.at[k, segment(where_ref, r)],
                 sems.at[k, r],
             )
@@ -457,7 +465,7 @@
                 copy.start()
 
     for k in range(2):
-        for copy in load(e, k):
+        for copy in load(0, k):
             copy.wait()
         for n in range(H // 256):
             columns = slice(n * 256, (n + 1) * 256)
@@ -515,7 +523,7 @@
         grid_spec=pltpu.PrefetchScalarGridSpec(
             num_scalar_prefetch=2,
             grid=(2,),
-            in_specs=[any_spec] * 5 + ins,
+            in_specs=[any_spec] * 7 + ins,
             out_specs=outs,
             scratch_shapes=[
                 pltpu.VMEM((2, SLOTS, 1024), jnp.bfloat16),
@@ -612,8 +620,9 @@
     gate, up = gate_values[0], up_values[0]
 
     def send(rows, before):
+        along = (0, 1, 1, 2, 2, 3)
         return [rows[0]] + [
-            move(after(rows[i], *before), False, SHIFTS[i], 0) for i in range(1, 4)
+            move(after(rows[i], *before), False, SHIFTS[along[i]], 0) for i in range(1, 6)
         ]
 
     rows = pick(1, after(held, factor, share), blocks)
@@ -636,7 +645,7 @@
     own = send(rows, sent[1:])
     theirs = partial(False, where, their_weighted, sent)[0]
     before = grads(0, after(where, theirs), factor, effective, sent)[0]
-    theirs = lax.psum_scatter(theirs, "dp", scatter_dimension=0, tiled=False)
+    theirs = lax.psum_scatter(after(theirs, own[1], own[3]), "dp", scatter_dimension=0, tiled=False)
     before = swap(after(before, *own[1:]))
     ours = exchange(partial(True, where, weighted, own))
     grad_gate, grad_up, scores = grads(
@@ -647,7 +656,7 @@
         scores.reshape(2, SLOTS), "expert", split_axis=1, concat_axis=0, tiled=True
     )
     grad_route = back(expert_ids, rank, returned)
-    summed = swap(theirs)
+    summed = swap(after(theirs, scores))
     grad_down = finish(where, factor, summed, ours)
     return (grad_gate[None], grad_up[None], grad_down, grad_route)
 

time: 311 us -> 302 us (0.971)
  waiting for transfers between devices: 111 us -> 89.7 us
  local copies, waits for them, and re-layouts: 6.5 us -> 13.3 us
  starting transfers between devices: 36.3 us -> 41.4 us
    ppermute x15 -> x19, waiting for transfers between devices: 99.7 us -> 79.9 us  [on_device(): move = lambda value, *to: lax.ppermute(value, 'expert', pairs(*to))]
    unnamed x26 -> x34, local copies, waits for them, and re-layouts: 2.19 us -> 7.57 us
    ppermute x15 -> x19, starting transfers between devices: 18.8 us -> 23.7 us  [on_device(): move = lambda value, *to: lax.ppermute(value, 'expert', pairs(*to))]
  transfers between devices with their start and end apart: 25 -> 29, of which waited for: 12 -> 10; matrix products, arithmetic and copies ran while one was open for 2% -> 3% of each run, Pallas kernels for 34% -> 35%
where the time goes in v1:
time: 302 us; the launch traced here: 301 us
  Pallas kernels  120 us (40%)
  waiting for transfers between devices  89.7 us (30%)
  starting transfers between devices  41.4 us (14%)
  blocking collectives  14.5 us (5%)
  between operations  14.5 us (5%)
  local copies, waits for them, and re-layouts  13.3 us (4%)
  other arithmetic  6.87 us (2%)
    ppermute x19, waiting for transfers between devices, on_device(): move = lambda value, *to: lax.ppermute(value, 'expert', pairs(*to))  79.9 us
    pallas_call x2, Pallas kernels, grads(): pl.pallas_call(functools.partial(grads_kernel, group), grid_spec=pltpu.Pr...  42.2 us
    pallas_call x2, Pallas kernels, partial(): pl.pallas_call(functools.partial(partial_kernel, ring), grid_spec=pltpu.P...  27.4 us
    ppermute x19, starting transfers between devices, on_device(): move = lambda value, *to: lax.ppermute(value, 'expert', pairs(*to))  23.7 us
    pallas_call x2, Pallas kernels, pick(): pl.pallas_call(functools.partial(pick_kernel, swap), grid_spec=pltpu.Pref...  19.9 us
    all_to_all x1, blocking collectives, on_device(): lax.all_to_all(scores.reshape(2, SLOTS), 'expert', split_axis=1, concat_a...  14.5 us
    pallas_call x2, Pallas kernels, shrink(): pl.pallas_call(shrink_kernel, grid_spec=pltpu.PrefetchScalarGridSpec(num_...  9.82 us
    pallas_call x1, Pallas kernels, weigh(): pl.pallas_call(weigh_kernel, grid_spec=pltpu.PrefetchScalarGridSpec(num_s...  9.25 us
  transfers between devices with their start and end apart: 29, of which 10 were waited for; matrix products, arithmetic and copies ran while one was open for 3% of the time, Pallas kernels for 35%

profile of v1, /device:TPU:1, one launch (start us, length us, event | category | flops | bytes accessed | tf_op | source)
XLA Modules:
  0.0 300.7 jit_solution(10023883828294774558)
XLA Ops:
  7.2 1.3 convert_bitcast_fusion.1.weights_ref
  8.5 4.4 %split.1 = (bf16[2,272,2048]{2,1,0:T(8,128)(2,1)}, bf16[272,2048]{1,0:T(8,128)(2,1)}, bf16[64,128]{1,0:T(8,128)(2,1)}, f32[64,256]{1,0:T(8,128)}) custom-call(s32[1]{0:T(128)} %bitcast.4.core_ref.half_ref, bf16[256,4096]{1,0:T(8,128)(2,1)} %rows_ref.1, s32[8,256]{1,0:T(8,128)} %bitcast.54, f32[8,256]{1,0:T(8,128)} %convert_bitcast_fusion.1.weights_ref), custom_call_target="tpu_custom_call" | custom-call | tf_op jit(solution)/shard_map/split/pallas_call | solution.py:164
  12.9 4.9 %shrink.2 = (bf16[2,768,512]{2,1,0:T(8,128)(2,1)}, f32[2,2,2,8,128]{4,3,2,1,0:T(8,128)}) custom-call(s32[1]{0:T(128)} %bitcast.6.half_ref, bf16[2,768,1024]{2,1,0:T(8,128)(2,1)} %w_ref.1), custom_call_target="tpu_custom_call" | custom-call | flops 23592960 | bytes 3145728 | tf_op jit(solution)/shard_map/shrink/pallas_call | solution.py:86
  17.8 1.4 collective-permute-start.3
  19.2 4.9 %shrink.3 = (bf16[2,2,768,512]{3,2,1,0:T(8,128)(2,1)}, f32[2,2,2,8,128]{4,3,2,1,0:T(8,128)}) custom-call(s32[1]{0:T(128)} %bitcast.4.core_ref.half_ref, bf16[2,768,1024]{2,1,0:T(8,128)(2,1)} %w_ref.1), custom_call_target="tpu_custom_call" | custom-call | flops 23592960 | bytes 3145728 | tf_op jit(solution)/shard_map/shrink/pallas_call | solution.py:86
  24.2 1.2 bitcast_dynamic-update-slice_fusion
  25.5 2.9 collective-permute-done.4
  28.6 2.6 collective-permute-start.6
  31.3 24.4 %collective-permute-done.6.refs_2_ = bf16[2,272,2048]{2,1,0:T(8,128)(2,1)S(1)} collective-permute-done((bf16[2,272,2048]{2,1,0:T(8,128)(2,1)S(1)}, bf16[2,272,2048]{2,1,0:T(8,128)(2,1)S(1)}, u32[]{:S(2)}, u32[]{:S(2)}) %collective-permute-start.6) | collective-permute-done | bytes 2228256 | tf_op jit(solution)/shard_map/ppermute | solution.py:593
  55.7 3.6 %collective-permute-start.8 = (bf16[272,2048]{1,0:T(8,128)(2,1)S(1)}, bf16[272,2048]{1,0:T(8,128)(2,1)}, u32[]{:S(2)}, u32[]{:S(2)}) collective-permute-start(bf16[272,2048]{1,0:T(8,128)(2,1)S(1)} %slice_bitcast_fusion), channel_id=1, source_target_pairs={{0,24},{1,7},{2,26},{3,1},{4,28},{5,3},{6,30},{7,5},{8,0},{9,15},{... | collective-permute-start | bytes 3342344 | tf_op jit(solution)/shard_map/ppermute | solution.py:593
  59.5 1.2 copy-done.11
  60.8 2.8 collective-permute-start.2
  63.6 8.6 %all-to-all-start = ((bf16[32,2,36]{2,1,0:T(2,128)(2,1)}), bf16[32,2,36]{2,1,0:T(2,128)(2,1)S(1)}, u32[]{:S(2)}, u32[]{:S(2)}) async-start(bf16[32,2,36]{2,1,0:T(2,128)(2,1)} %bitcast.19), calls=%async_computation | async-start | bytes 32768 | tf_op jit(solution)/shard_map/all_to_all | solution.py:610
  73.4 4.0 %collective-permute-done.1 = f32[2,2]{1,0:T(2,128)S(1)} collective-permute-done((f32[2,2]{1,0:T(2,128)S(1)}, f32[2,2]{1,0:T(2,128)S(1)}, u32[]{:S(2)}, u32[]{:S(2)}) %collective-permute-start.1) | collective-permute-done | bytes 48 | tf_op jit(solution)/shard_map/ppermute | solution.py:595
  77.4 0.8 fusion.2.factor_ref
  78.2 1.0 all-to-all-done
  79.2 1.0 copy-done.16
  80.2 9.9 %pick0.1 = (bf16[2,288,2048]{2,1,0:T(8,128)(2,1)}, bf16[288,2048]{1,0:T(8,128)(2,1)}, bf16[288,2048]{1,0:T(8,128)(2,1)}, bf16[288,2048]{1,0:T(8,128)(2,1)}, bf16...) custom-call(s32[10]{0:T(128)} %stack.65.where_ref, bf16[2,272,2048]{2,1,0:T(8,128)(2,1)} %copy-done.15, ...), custom_call_target="tpu_custom_call" | custom-call | flops 4831838208 | bytes 17825792 | tf_op jit(solution)/shard_map/pick0/pallas_call | solution.py:265
  90.1 2.0 collective-permute-start.13
  92.1 0.9 collective-permute-start.12
  93.5 1.0 collective-permute-start.10
  95.1 10.0 %pick1.1 = (bf16[2,288,2048]{2,1,0:T(8,128)(2,1)}, bf16[288,2048]{1,0:T(8,128)(2,1)}, bf16[288,2048]{1,0:T(8,128)(2,1)}, bf16[288,2048]{1,0:T(8,128)(2,1)}, bf16...) custom-call(s32[10]{0:T(128)} %stack.65.where_ref, bf16[2,272,2048]{2,1,0:T(8,128)(2,1)} %copy-done.15, ...), custom_call_target="tpu_custom_call" | custom-call | flops 4831838208 | bytes 17825792 | tf_op jit(solution)/shard_map/pick1/pallas_call | solution.py:265
  105.7 2.1 reshape.40.weight_ref.refs_9_
  107.8 9.2 %weigh.1 = (bf16[2,768,1152]{2,1,0:T(8,128)(2,1)}, bf16[2,768,1152]{2,1,0:T(8,128)(2,1)}) custom-call(s32[1]{0:T(128)} %bitcast.4.core_ref.half_ref, bf16[2,1152,768]{2,1,0:T(8,128)(2,1)} %bitcast.48, bf16[2,1152,768]{2,1,0:T(8,128)(2,1)} %bitcast.50, f32[2,1152,1]{2,1,0:T(8,128)} %reshape.40.weight_ref.refs_9_), custom_call_target="tpu_custom_call" | custom-call | flops 35389440 | bytes 14155776 | tf_op jit(solution)/shard_map/weigh/pallas_call | solution.py:320
  117.1 14.9 %collective-permute-done.12.refs_4_ = bf16[288,2048]{1,0:T(8,128)(2,1)S(1)} collective-permute-done((bf16[288,2048]{1,0:T(8,128)(2,1)}, bf16[288,2048]{1,0:T(8,128)(2,1)S(1)}, u32[]{:S(2)}, u32[]{:S(2)}) %collective-permute-start.12) | collective-permute-done | bytes 1179680 | tf_op jit(solution)/shard_map/ppermute | solution.py:593
  132.0 12.6 %collective-permute-done.11.refs_3_ = bf16[288,2048]{1,0:T(8,128)(2,1)} collective-permute-done((bf16[288,2048]{1,0:T(8,128)(2,1)}, bf16[288,2048]{1,0:T(8,128)(2,1)}, u32[]{:S(2)}, u32[]{:S(2)}) %collective-permute-start.11) | collective-permute-done | bytes 1179680 | tf_op jit(solution)/shard_map/ppermute | solution.py:593
  145.3 1.5 collective-permute-start.19
  147.6 1.9 collective-permute-start.16
  150.2 2.8 collective-permute-done.19.weighted_ref
  153.0 13.7 %partial.2 = bf16[4,2,2,768,256]{4,3,2,1,0:T(8,128)(2,1)} custom-call(s32[6]{0:T(128)} %stack.56.where_ref, bf16[2,768,1152]{2,1,0:T(8,128)(2,1)} %collective-permute-done.19.weighted_ref, bf16[2,288,2048]{2,1,0:T(8,128)(2,1)} %get-tuple-element.61.refs_0_, bf16[288,2048]{1,0:T(8,128)(2,1)} %collective-permute-done.9.refs_1_, ...), custom_call_target="tpu_custom_call" | custom-call | flops 7247757312 | bytes 19267584 | tf_op jit(solution)/shard_map/partial/pallas_call | solution.py:414
  166.7 2.3 collective-permute-start.18
  169.4 2.3 collective-permute-start.17
  171.7 16.0 %grads0.1 = f32[2,1152,768]{2,1,0:T(8,128)} custom-call(s32[6]{0:T(128)} %stack.56.where_ref, f32[2]{0:T(128)} %fusion.2.factor_ref, bf16[4,2,2,768,512]{4,3,2,1,0:T(8,128)(2,1)} %all-gather.2.cloned.1.call-done.effective_ref, bf16[2,288,2048]{2,1,0:T(8,128)(2,1)} %get-tuple-element.61.refs_0_, bf16[288,2048]{1,0:T(8,128)(2,1)} %collective-permute-done.9.refs_1_, ...), custom_call_target="tpu_custom_call" | custom-call | flops 7247757312 | bytes 22806528 | tf_op jit(solution)/shard_map/grads0/pallas_call | solution.py:521
  187.7 21.5 %collective-permute-done.15.refs_2_ = bf16[288,2048]{1,0:T(8,128)(2,1)S(1)} collective-permute-done((bf16[288,2048]{1,0:T(8,128)(2,1)}, bf16[288,2048]{1,0:T(8,128)(2,1)S(1)}, u32[]{:S(2)}, u32[]{:S(2)}) %collective-permute-start.15) | collective-permute-done | bytes 1179680 | tf_op jit(solution)/shard_map/ppermute | solution.py:593
  209.3 1.1 copy-done.5
  210.4 1.1 collective-permute-start.20
  211.5 13.7 %partial.3 = (bf16[2,2,768,256]{3,2,1,0:T(8,128)(2,1)}, bf16[2,2,768,256]{3,2,1,0:T(8,128)(2,1)}, bf16[2,2,768,256]{3,2,1,0:T(8,128)(2,1)}, bf16[2,768,256]{2,1,0:T(8,128)(2,1)}, bf16[2,768,256]{2,1,0:T(8,128)(2,1)}) custom-call(s32[6]{0:T(128)} %stack.56.where_ref, bf16[2,768,1152]{2,1,0:T(8,128)(2,1)} %get-tuple-element.89.weighted_ref, ...), custom_call_target="tpu_custom_call" | custom-call | flops 7247757312 | bytes 19267584 | tf_op jit(solution)/shard_map/partial/pallas_call | solution.py:414
  226.0 2.6 collective-permute-start.23
  228.6 2.8 copy-done
  231.4 26.2 %grads1.1 = (bf16[2,1152,768]{2,1,0:T(8,128)(2,1)}, bf16[2,1152,768]{2,1,0:T(8,128)(2,1)}, f32[2,1152,1]{2,1,0:T(8,128)}) custom-call(s32[6]{0:T(128)} %stack.56.where_ref, f32[2]{0:T(128)} %fusion.2.factor_ref, bf16[4,2,2,768,512]{4,3,2,1,0:T(8,128)(2,1)} %all-gather.2.cloned.1.call-done.effective_ref, bf16[2,288,2048]{2,1,0:T(8,128)(2,1)} %get-tuple-element.68.refs_0_, ...), custom_call_target="tpu_custom_call" | custom-call | flops 7300841472 | bytes 36962304 | tf_op jit(solution)/shard_map/grads1/pallas_call | solution.py:521
  258.3 4.7 %collective-permute-done.22.refs_1_ = bf16[2,2,768,256]{3,2,1,0:T(8,128)(2,1)} collective-permute-done((bf16[2,2,768,256]{3,2,1,0:T(8,128)(2,1)}, bf16[2,2,768,256]{3,2,1,0:T(8,128)(2,1)}, u32[]{:S(2)}, u32[]{:S(2)}) %collective-permute-start.22) | collective-permute-done | bytes 1572896 | tf_op jit(solution)/shard_map/ppermute | solution.py:595
  263.1 2.1 fusion.1
  265.2 2.2 fusion
  267.4 2.6 collective-permute-start.25
  270.5 14.5 %all_to_all.24 = f32[2,32,36]{2,0,1:T(2,128)} all-to-all(f32[2,32,36]{2,0,1:T(2,128)S(1)} %copy.23), channel_id=1, replica_groups=mesh['dp'=4,'expert'=32] {'expert'}, dimensions={1} | all-to-all | bytes 18432 | tf_op jit(solution)/shard_map/all_to_all | solution.py:655
  285.0 2.0 back.1
  287.0 0.9 copy-done.7
  288.4 5.5 %finish.1 = bf16[2,768,1024]{2,1,0:T(8,128)(2,1)} custom-call(s32[6]{0:T(128)} %stack.56.where_ref, f32[2]{0:T(128)} %fusion.2.factor_ref, bf16[2,2,768,256]{3,2,1,0:T(8,128)(2,1)} %copy-done.2, bf16[2,2,768,256]{3,2,1,0:T(8,128)(2,1)} %get-tuple-element.90.refs_0_, bf16[2,2,768,256]{3,2,1,0:T(8,128)(2,1)} %collective-permute-done.22.refs_1_, ...), custom_call_target="tpu_custom_call" | custom-call | tf_op jit(solution)/shard_map/finish/pallas_call | solution.py:569
  (77 shorter events, 8.3 us)
Async XLA Ops:
  7.2 164.6 %all-gather.2.cloned.1.call-start = ((), (), s32[]{:S(2)}) async-start(), calls=%async_computation.3 | async-start | bytes 15728640 | tf_op jit(solution)/shard_map/all_gather | solution.py:607
  17.8 6.3 %collective-permute-start.3 = (bf16[2,768,512]{2,1,0:T(8,128)(2,1)}, bf16[2,768,512]{2,1,0:T(8,128)(2,1)S(1)}, u32[]{:S(2)}, u32[]{:S(2)}) collective-permute-start(bf16[2,768,512]{2,1,0:T(8,128)(2,1)} %get-tuple-element.56), channel_id=1, source_target_pairs={{0,1},{1,0},{2,3},{3,2},{4,5},{5,4},{6,7},{7,6},{8,9},{9,8},{10,11... | collective-permute-start | bytes 4718600 | tf_op jit(solution)/shard_map/ppermute | solution.py:593
  25.4 3.1 %copy-start.14 = (bf16[2,272,2048]{2,1,0:T(8,128)(2,1)S(1)}, bf16[2,272,2048]{2,1,0:T(8,128)(2,1)}, u32[]{:S(2)}) copy-start(bf16[2,272,2048]{2,1,0:T(8,128)(2,1)} %get-tuple-element.59) | copy-start | bytes 6684676
  25.4 3.0 %collective-permute-start.4 = (bf16[272,2048]{1,0:T(8,128)(2,1)}, bf16[272,2048]{1,0:T(8,128)(2,1)S(1)}, u32[]{:S(2)}, u32[]{:S(2)}) collective-permute-start(bf16[272,2048]{1,0:T(8,128)(2,1)} %get-tuple-element.51), channel_id=1, source_target_pairs={{0,1},{1,0},{2,3},{3,2},{4,5},{5,4},{6,7},{7,6},{8,9},{9,8},{10,11... | collective-permute-start | bytes 3342344 | tf_op jit(solution)/shard_map/ppermute | solution.py:593
  28.6 30.7 %copy-start.15 = (bf16[2,272,2048]{2,1,0:T(8,128)(2,1)}, bf16[2,272,2048]{2,1,0:T(8,128)(2,1)S(1)}, u32[]{:S(2)}) copy-start(bf16[2,272,2048]{2,1,0:T(8,128)(2,1)S(1)} %bitcast_dynamic-update-slice_fusion.1.refs_0_) | copy-start | bytes 6684676
  28.6 27.0 %collective-permute-start.6 = (bf16[2,272,2048]{2,1,0:T(8,128)(2,1)S(1)}, bf16[2,272,2048]{2,1,0:T(8,128)(2,1)S(1)}, u32[]{:S(2)}, u32[]{:S(2)}) collective-permute-start(bf16[2,272,2048]{2,1,0:T(8,128)(2,1)S(1)} %bitcast_dynamic-update-slice_fusion.1.refs_0_), channel_id=1, source_target_pairs={{0,24},{1,7},{2,26},{3,1},{4,28},{5,3},{6,30},{7,5},{8,0},{9,15},{... | collective-permute-start | bytes 6684680 | tf_op jit(solution)/shard_map/ppermute | solution.py:593
  31.3 28.1 %collective-permute-start.5 = (bf16[2,272,2048]{2,1,0:T(8,128)(2,1)S(1)}, bf16[2,272,2048]{2,1,0:T(8,128)(2,1)S(1)}, u32[]{:S(2)}, u32[]{:S(2)}) collective-permute-start(bf16[2,272,2048]{2,1,0:T(8,128)(2,1)S(1)} %bitcast_dynamic-update-slice_fusion.1.refs_0_), channel_id=1, source_target_pairs={{0,8},{1,3},{2,10},{3,5},{4,12},{5,7},{6,14},{7,1},{8,16},{9,11},{... | collective-permute-start | bytes 6684680 | tf_op jit(solution)/shard_map/ppermute | solution.py:593
  55.6 3.8 %copy-start.10 = (bf16[2,272,2048]{2,1,0:T(8,128)(2,1)}, bf16[2,272,2048]{2,1,0:T(8,128)(2,1)S(1)}, u32[]{:S(2)}) copy-start(bf16[2,272,2048]{2,1,0:T(8,128)(2,1)S(1)} %collective-permute-done.6.refs_2_) | copy-start | bytes 6684676
  55.7 5.0 %copy-start.12 = (f32[2,2,2,8,128]{4,3,2,1,0:T(8,128)S(1)}, f32[2,2,2,8,128]{4,3,2,1,0:T(8,128)}, u32[]{:S(2)}) copy-start(f32[2,2,2,8,128]{4,3,2,1,0:T(8,128)} %get-tuple-element.53) | copy-start | bytes 98308
  55.7 5.0 %copy-start.13 = (f32[2,2,2,8,128]{4,3,2,1,0:T(8,128)S(1)}, f32[2,2,2,8,128]{4,3,2,1,0:T(8,128)}, u32[]{:S(2)}) copy-start(f32[2,2,2,8,128]{4,3,2,1,0:T(8,128)} %get-tuple-element.54) | copy-start | bytes 98308
  55.7 23.4 %collective-permute-start.8 = (bf16[272,2048]{1,0:T(8,128)(2,1)S(1)}, bf16[272,2048]{1,0:T(8,128)(2,1)}, u32[]{:S(2)}, u32[]{:S(2)}) collective-permute-start(bf16[272,2048]{1,0:T(8,128)(2,1)S(1)} %slice_bitcast_fusion), channel_id=1, source_target_pairs={{0,24},{1,7},{2,26},{3,1},{4,28},{5,3},{6,30},{7,5},{8,0},{9,15},{... | collective-permute-start | bytes 3342344 | tf_op jit(solution)/shard_map/ppermute | solution.py:593
  59.3 1.4 copy-start.11
  59.4 19.7 %collective-permute-start.7 = (bf16[272,2048]{1,0:T(8,128)(2,1)S(1)}, bf16[272,2048]{1,0:T(8,128)(2,1)S(1)}, u32[]{:S(2)}, u32[]{:S(2)}) collective-permute-start(bf16[272,2048]{1,0:T(8,128)(2,1)S(1)} %slice_bitcast_fusion.1), channel_id=1, source_target_pairs={{0,8},{1,3},{2,10},{3,5},{4,12},{5,7},{6,14},{7,1},{8,16},{9,11},{... | collective-permute-start | bytes 3342344 | tf_op jit(solution)/shard_map/ppermute | solution.py:593
  60.8 12.6 %collective-permute-start.2 = (f32[2,2]{1,0:T(2,128)S(1)}, f32[2,2]{1,0:T(2,128)S(1)}, u32[]{:S(2)}, u32[]{:S(2)}) collective-permute-start(f32[2,2]{1,0:T(2,128)S(1)} %add_reduce_fusion), channel_id=1, source_target_pairs={{0,96},{32,0},{64,32},{96,64},{1,97},{33,1},{65,33},{97,65},{2,98}... | collective-permute-start | bytes 56 | tf_op jit(solution)/shard_map/ppermute | solution.py:596
  63.6 9.5 %collective-permute-start = (f32[2,2]{1,0:T(2,128)S(1)}, f32[2,2]{1,0:T(2,128)S(1)}, u32[]{:S(2)}, u32[]{:S(2)}) collective-permute-start(f32[2,2]{1,0:T(2,128)S(1)} %add_reduce_fusion), channel_id=1, source_target_pairs={{0,32},{32,64},{64,96},{96,0},{1,33},{33,65},{65,97},{97,1},{2,34}... | collective-permute-start | bytes 56 | tf_op jit(solution)/shard_map/ppermute | solution.py:595
  63.6 15.6 %all-to-all-start = ((bf16[32,2,36]{2,1,0:T(2,128)(2,1)}), bf16[32,2,36]{2,1,0:T(2,128)(2,1)S(1)}, u32[]{:S(2)}, u32[]{:S(2)}) async-start(bf16[32,2,36]{2,1,0:T(2,128)(2,1)} %bitcast.19), calls=%async_computation | async-start | bytes 32768 | tf_op jit(solution)/shard_map/all_to_all | solution.py:610
  72.2 185.4 %reduce-scatter.2.cloned.1.call-start = ((), (), s32[]{:S(2)}) async-start(), calls=%async_computation.4 | async-start | bytes 7864320 | tf_op jit(solution)/shard_map/reduce_scatter | solution.py:648
  73.1 4.3 %collective-permute-start.1 = (f32[2,2]{1,0:T(2,128)S(1)}, f32[2,2]{1,0:T(2,128)S(1)}, u32[]{:S(2)}, u32[]{:S(2)}) collective-permute-start(f32[2,2]{1,0:T(2,128)S(1)} %collective-permute-done), channel_id=1, source_target_pairs={{0,32},{32,64},{64,96},{96,0},{1,33},{33,65},{65,97},{97,1},{2,34}... | collective-permute-start | bytes 56 | tf_op jit(solution)/shard_map/ppermute | solution.py:595
  79.2 1.0 copy-start.16
  90.1 55.2 %collective-permute-start.13 = (bf16[2,288,2048]{2,1,0:T(8,128)(2,1)}, bf16[2,288,2048]{2,1,0:T(8,128)(2,1)S(1)}, u32[]{:S(2)}, u32[]{:S(2)}) collective-permute-start(bf16[2,288,2048]{2,1,0:T(8,128)(2,1)} %get-tuple-element.66), channel_id=1, source_target_pairs={{0,4},{1,17},{2,6},{3,19},{4,0},{5,21},{6,2},{7,23},{8,12},{9,25},... | collective-permute-start | bytes 7077896 | tf_op jit(solution)/shard_map/ppermute | solution.py:593
  92.1 39.8 %collective-permute-start.12 = (bf16[288,2048]{1,0:T(8,128)(2,1)}, bf16[288,2048]{1,0:T(8,128)(2,1)S(1)}, u32[]{:S(2)}, u32[]{:S(2)}) collective-permute-start(bf16[288,2048]{1,0:T(8,128)(2,1)} %get-tuple-element.65), channel_id=1, source_target_pairs={{0,6},{1,25},{2,0},{3,27},{4,2},{5,29},{6,4},{7,31},{8,14},{9,1},{... | collective-permute-start | bytes 3538952 | tf_op jit(solution)/shard_map/ppermute | solution.py:593
  93.0 51.6 %collective-permute-start.11 = (bf16[288,2048]{1,0:T(8,128)(2,1)}, bf16[288,2048]{1,0:T(8,128)(2,1)}, u32[]{:S(2)}, u32[]{:S(2)}) collective-permute-start(bf16[288,2048]{1,0:T(8,128)(2,1)} %get-tuple-element.64), channel_id=1, source_target_pairs={{0,6},{1,25},{2,0},{3,27},{4,2},{5,29},{6,4},{7,31},{8,14},{9,1},{... | collective-permute-start | bytes 3538952 | tf_op jit(solution)/shard_map/ppermute | solution.py:593
  93.5 51.2 %collective-permute-start.10 = (bf16[288,2048]{1,0:T(8,128)(2,1)}, bf16[288,2048]{1,0:T(8,128)(2,1)}, u32[]{:S(2)}, u32[]{:S(2)}) collective-permute-start(bf16[288,2048]{1,0:T(8,128)(2,1)} %get-tuple-element.63), channel_id=1, source_target_pairs={{0,2},{1,9},{2,4},{3,11},{4,6},{5,13},{6,0},{7,15},{8,10},{9,17},{... | collective-permute-start | bytes 3538952 | tf_op jit(solution)/shard_map/ppermute | solution.py:593
  94.5 50.8 %collective-permute-start.9 = (bf16[288,2048]{1,0:T(8,128)(2,1)}, bf16[288,2048]{1,0:T(8,128)(2,1)}, u32[]{:S(2)}, u32[]{:S(2)}) collective-permute-start(bf16[288,2048]{1,0:T(8,128)(2,1)} %get-tuple-element.62), channel_id=1, source_target_pairs={{0,2},{1,9},{2,4},{3,11},{4,6},{5,13},{6,0},{7,15},{8,10},{9,17},{... | collective-permute-start | bytes 3538952 | tf_op jit(solution)/shard_map/ppermute | solution.py:593
  132.0 21.0 %copy-start.3 = (bf16[288,2048]{1,0:T(8,128)(2,1)}, bf16[288,2048]{1,0:T(8,128)(2,1)S(1)}, u32[]{:S(2)}) copy-start(bf16[288,2048]{1,0:T(8,128)(2,1)S(1)} %collective-permute-done.12.refs_4_) | copy-start | bytes 3538948
  145.3 7.7 %copy-start.1 = (bf16[2,288,2048]{2,1,0:T(8,128)(2,1)}, bf16[2,288,2048]{2,1,0:T(8,128)(2,1)S(1)}, u32[]{:S(2)}) copy-start(bf16[2,288,2048]{2,1,0:T(8,128)(2,1)S(1)} %collective-permute-done.13.refs_5_) | copy-start | bytes 7077892
  145.3 7.7 %collective-permute-start.19 = (bf16[2,768,1152]{2,1,0:T(8,128)(2,1)}, bf16[2,768,1152]{2,1,0:T(8,128)(2,1)}, u32[]{:S(2)}, u32[]{:S(2)}) collective-permute-start(bf16[2,768,1152]{2,1,0:T(8,128)(2,1)} %get-tuple-element.81), channel_id=1, source_target_pairs={{0,1},{1,0},{2,3},{3,2},{4,5},{5,4},{6,7},{7,6},{8,9},{9,8},{10,11... | collective-permute-start | bytes 10616840 | tf_op jit(solution)/shard_map/ppermute | solution.py:593
  146.8 19.9 %collective-permute-start.14 = (bf16[288,2048]{1,0:T(8,128)(2,1)}, bf16[288,2048]{1,0:T(8,128)(2,1)}, u32[]{:S(2)}, u32[]{:S(2)}) collective-permute-start(bf16[288,2048]{1,0:T(8,128)(2,1)} %get-tuple-element.70), channel_id=1, source_target_pairs={{0,2},{1,9},{2,4},{3,11},{4,6},{5,13},{6,0},{7,15},{8,10},{9,17},{... | collective-permute-start | bytes 3538952 | tf_op jit(solution)/shard_map/ppermute | solution.py:593
  147.6 19.1 %collective-permute-start.16 = (bf16[288,2048]{1,0:T(8,128)(2,1)}, bf16[288,2048]{1,0:T(8,128)(2,1)}, u32[]{:S(2)}, u32[]{:S(2)}) collective-permute-start(bf16[288,2048]{1,0:T(8,128)(2,1)} %get-tuple-element.74), channel_id=1, source_target_pairs={{0,6},{1,25},{2,0},{3,27},{4,2},{5,29},{6,4},{7,31},{8,14},{9,1},{... | collective-permute-start | bytes 3538952 | tf_op jit(solution)/shard_map/ppermute | solution.py:593
  166.7 43.7 %collective-permute-start.18 = (bf16[2,288,2048]{2,1,0:T(8,128)(2,1)}, bf16[2,288,2048]{2,1,0:T(8,128)(2,1)}, u32[]{:S(2)}, u32[]{:S(2)}) collective-permute-start(bf16[2,288,2048]{2,1,0:T(8,128)(2,1)} %get-tuple-element.78), channel_id=1, source_target_pairs={{0,4},{1,17},{2,6},{3,19},{4,0},{5,21},{6,2},{7,23},{8,12},{9,25},... | collective-permute-start | bytes 7077896 | tf_op jit(solution)/shard_map/ppermute | solution.py:593
  169.1 40.2 %collective-permute-start.15 = (bf16[288,2048]{1,0:T(8,128)(2,1)}, bf16[288,2048]{1,0:T(8,128)(2,1)S(1)}, u32[]{:S(2)}, u32[]{:S(2)}) collective-permute-start(bf16[288,2048]{1,0:T(8,128)(2,1)} %get-tuple-element.72), channel_id=1, source_target_pairs={{0,2},{1,9},{2,4},{3,11},{4,6},{5,13},{6,0},{7,15},{8,10},{9,17},{... | collective-permute-start | bytes 3538952 | tf_op jit(solution)/shard_map/ppermute | solution.py:593
  169.4 39.9 %collective-permute-start.17 = (bf16[288,2048]{1,0:T(8,128)(2,1)}, bf16[288,2048]{1,0:T(8,128)(2,1)S(1)}, u32[]{:S(2)}, u32[]{:S(2)}) collective-permute-start(bf16[288,2048]{1,0:T(8,128)(2,1)} %get-tuple-element.76), channel_id=1, source_target_pairs={{0,6},{1,25},{2,0},{3,27},{4,2},{5,29},{6,4},{7,31},{8,14},{9,1},{... | collective-permute-start | bytes 3538952 | tf_op jit(solution)/shard_map/ppermute | solution.py:593
  209.2 2.3 copy-start.4
  209.3 1.1 copy-start.5
  210.4 18.2 %collective-permute-start.20 = (f32[2,1152,768]{2,1,0:T(8,128)}, f32[2,1152,768]{2,1,0:T(8,128)S(1)}, u32[]{:S(2)}, u32[]{:S(2)}) collective-permute-start(f32[2,1152,768]{2,1,0:T(8,128)} %grads0.1), channel_id=1, source_target_pairs={{0,1},{1,0},{2,3},{3,2},{4,5},{5,4},{6,7},{7,6},{8,9},{9,8},{10,11... | collective-permute-start | bytes 21233672 | tf_op jit(solution)/shard_map/ppermute | solution.py:593
  225.2 37.8 %collective-permute-start.22 = (bf16[2,2,768,256]{3,2,1,0:T(8,128)(2,1)}, bf16[2,2,768,256]{3,2,1,0:T(8,128)(2,1)}, u32[]{:S(2)}, u32[]{:S(2)}) collective-permute-start(bf16[2,2,768,256]{3,2,1,0:T(8,128)(2,1)} %get-tuple-element.91), channel_id=1, source_target_pairs={{0,32},{32,64},{64,96},{96,0},{1,33},{33,65},{65,97},{97,1},{2,34}... | collective-permute-start | bytes 4718600 | tf_op jit(solution)/shard_map/ppermute | solution.py:595
  226.0 37.1 %copy-start.9 = (bf16[2,768,256]{2,1,0:T(8,128)(2,1)S(1)}, bf16[2,768,256]{2,1,0:T(8,128)(2,1)}, u32[]{:S(2)}) copy-start(bf16[2,768,256]{2,1,0:T(8,128)(2,1)} %get-tuple-element.94) | copy-start | bytes 2359300
  226.0 39.2 %collective-permute-start.23 = (bf16[2,2,768,256]{3,2,1,0:T(8,128)(2,1)}, bf16[2,2,768,256]{3,2,1,0:T(8,128)(2,1)}, u32[]{:S(2)}, u32[]{:S(2)}) collective-permute-start(bf16[2,2,768,256]{3,2,1,0:T(8,128)(2,1)} %get-tuple-element.92), channel_id=1, source_target_pairs={{0,96},{32,0},{64,32},{96,64},{1,97},{33,1},{65,33},{97,65},{2,98}... | collective-permute-start | bytes 4718600 | tf_op jit(solution)/shard_map/ppermute | solution.py:596
  228.6 2.8 copy-start
  257.7 7.5 %copy-start.8 = (bf16[2,768,256]{2,1,0:T(8,128)(2,1)S(1)}, bf16[2,768,256]{2,1,0:T(8,128)(2,1)}, u32[]{:S(2)}) copy-start(bf16[2,768,256]{2,1,0:T(8,128)(2,1)} %get-tuple-element.96) | copy-start | bytes 2359300
  257.7 29.3 %collective-permute-start.21 = (bf16[2,2,768,256]{3,2,1,0:T(8,128)(2,1)}, bf16[2,2,768,256]{3,2,1,0:T(8,128)(2,1)S(1)}, u32[]{:S(2)}, u32[]{:S(2)}) collective-permute-start(bf16[2,2,768,256]{3,2,1,0:T(8,128)(2,1)} %bitcast.59), channel_id=1, source_target_pairs={{0,1},{1,0},{2,3},{3,2},{4,5},{5,4},{6,7},{7,6},{8,9},{9,8},{10,11... | collective-permute-start | bytes 4718600 | tf_op jit(solution)/shard_map/ppermute | solution.py:593
  265.2 4.8 %copy-start.6 = (f32[2,1152,1]{2,1,0:T(8,128)S(1)}, f32[2,1152,1]{2,1,0:T(8,128)}, u32[]{:S(2)}) copy-start(f32[2,1152,1]{2,1,0:T(8,128)} %get-tuple-element.87) | copy-start | bytes 27652
  265.2 21.9 %collective-permute-start.24 = (bf16[2,768,256]{2,1,0:T(8,128)(2,1)}, bf16[2,768,256]{2,1,0:T(8,128)(2,1)S(1)}, u32[]{:S(2)}, u32[]{:S(2)}) collective-permute-start(bf16[2,768,256]{2,1,0:T(8,128)(2,1)} %fusion.1), channel_id=1, source_target_pairs={{0,32},{32,64},{64,96},{96,0},{1,33},{33,65},{65,97},{97,1},{2,34}... | collective-permute-start | bytes 2359304 | tf_op jit(solution)/shard_map/ppermute | solution.py:595
  267.4 19.6 %collective-permute-start.25 = (bf16[2,768,256]{2,1,0:T(8,128)(2,1)}, bf16[2,768,256]{2,1,0:T(8,128)(2,1)}, u32[]{:S(2)}, u32[]{:S(2)}) collective-permute-start(bf16[2,768,256]{2,1,0:T(8,128)(2,1)} %fusion), channel_id=1, source_target_pairs={{0,96},{32,0},{64,32},{96,64},{1,97},{33,1},{65,33},{97,65},{2,98}... | collective-permute-start | bytes 2359304 | tf_op jit(solution)/shard_map/ppermute | solution.py:596
  287.0 0.9 copy-start.7
  287.0 1.4 copy-start.2
Sparse Core Ops, SparseCore 0:
  25.5 120.5 all-gather.1
  166.8 63.2 reduce-scatter.1
